TPU v7x, 128 devices: a whole 4x4x4 slice. The times are simulated.
128 devices in a mesh: graph: 8 (over z, core), leaf: 16 (over y, x).
Axes of the slice: x: 4, y: 4, z: 4, core: 2. Of those that a mesh axis runs over, the one named last changes fastest.
Arguments:
- features: bfloat16 [1048576, 256], P(('graph', 'leaf')), may hold values from -6 to 6
- positions: float32 [3, 1048576], P(None, ('graph', 'leaf')), may hold values from -0.5 to 0.5
- energy_weight: float32 [1048576], P(('graph', 'leaf')), may hold values from -4 to 4
- send_slot: int32 [1048576], P(('graph', 'leaf')), may hold values from 0 to 8191, as said below
- tile_slot: int32 [1048576], P(('graph', 'leaf')), may hold values from 0 to 16383, as said below
- box_count: int32 [2048, 8], P('leaf', 'graph'), may hold values from 0 to 128, as said below
- list_box: int32 [2048, 64], P('leaf'), may hold values from 0 to 2047, as said below
- list_image: int32 [3, 2048, 64], P(None, 'leaf'), may hold values from -1 to 1
- w_in: bfloat16 [256, 256], replicated, may hold values from -0.375 to 0.375
- b_in: float32 [256], replicated, may hold values from -3 to 3
- w_mid: bfloat16 [256, 256], replicated, may hold values from -0.375 to 0.375
- b_mid: float32 [256], replicated, may hold values from -3 to 3
- w_out: bfloat16 [256], replicated, may hold values from -0.375 to 0.375
Outputs:
- feature_grad: bfloat16 [1048576, 256], P(('graph', 'leaf'))
- position_grad: float32 [3, 1048576], P(None, ('graph', 'leaf'))
- in_grad: float32 [256, 256], replicated
- in_bias_grad: float32 [256], replicated
- mid_grad: float32 [256, 256], replicated
- mid_bias_grad: float32 [256], replicated
- out_grad: float32 [256], replicated
Inputs may be any that keep to these rules, and one draw needn't show every extreme that they name: On each device send_slot is a permutation of 0 to 8191, so each device sends 64 atoms to every device. On each device the tile_slot values are distinct and are exactly the live slots b * 128 + k, k < box_count of that device's box b. `box_count`: the counts of one device sum to 8192. list_box[b, k] is the box at grid offset d_bk from box b, wrapped periodically, where d_bk has largest component magnitude exactly 2 and the 64 offsets of a box are distinct; list_image is the number of wraps along each dimension.
All inputs are finite; a program needn't handle non-finite values.
Results may differ from a plain program's by a relative error of at most 0.015.
Values may be sent and summed in bfloat16 or wider, within the bound.
A program may use at most 192 MiB of HBM per device.

v0:
```python
import jax
import jax.numpy as jnp
from jax import lax
from jax.sharding import PartitionSpec as P

SLOT_DEV = 128


coupling = 0.5


def silu_slope(pre_act):
    sigmoid_z = jax.nn.sigmoid(pre_act)
    return sigmoid_z * (1.0 + pre_act * (1.0 - sigmoid_z))


def box_coords(box_ids):
    return jnp.stack([box_ids % 8, box_ids // 8 % 8, box_ids // 64], 0).astype(jnp.float32)


def kernel_parts(separation):
    dist_sq = jnp.sum(separation * separation, 0)
    inverse = lax.rsqrt(dist_sq)
    return (inverse, inverse * inverse * inverse, dist_sq)


def translate(separation, sources):
    inverse, inverse_cube, dist_sq = kernel_parts(separation)
    projected = jnp.sum(separation * sources[1:], 0)
    potential_part = sources[0] * inverse - projected * inverse_cube
    gradient = (
        sources[0] * separation * inverse_cube
        + (sources[1:] - 3.0 * separation * projected / dist_sq) * inverse_cube
    )
    return jnp.concatenate([potential_part[None], gradient], 0)


def translate_back(separation, targets):
    inverse, inverse_cube, dist_sq = kernel_parts(separation)
    target_zero = targets[0][:, None]
    target_grad = targets[1:][:, :, None]
    projected = jnp.sum(separation * target_grad, 0)
    potential_part = target_zero * inverse + projected * inverse_cube
    gradient = (
        -target_zero * separation * inverse_cube
        + (target_grad - 3.0 * separation * projected / dist_sq) * inverse_cube
    )
    return jnp.concatenate([potential_part[None], gradient], 0)


def head_forward(row_block, w_in, b_in, w_mid, b_mid, w_out):
    pre_one = jnp.dot(row_block, w_in, preferred_element_type=jnp.float32) + b_in
    act_one = jax.nn.silu(pre_one).astype(jnp.bfloat16)
    pre_two = jnp.dot(act_one, w_mid, preferred_element_type=jnp.float32) + b_mid
    act_two = jax.nn.silu(pre_two).astype(jnp.bfloat16)
    charge = jnp.dot(act_two, w_out, preferred_element_type=jnp.float32)
    return (pre_one, act_one, pre_two, act_two, charge)


def head_backward(row_block, pre_one, act_one, pre_two, act_two, grad_bf, w_in, w_mid, w_out):
    contract_rows = (((0,), (0,)), ((), ()))
    contract_cols = (((1,), (1,)), ((), ()))
    out_grad = jnp.dot(grad_bf, act_two, preferred_element_type=jnp.float32)
    mid_slope = (
        grad_bf.astype(jnp.float32)[:, None] * w_out.astype(jnp.float32)[None] * silu_slope(pre_two)
    ).astype(jnp.bfloat16)
    mid_grad = lax.dot_general(
        act_one, mid_slope, contract_rows, preferred_element_type=jnp.float32
    )
    mid_bias = jnp.sum(mid_slope, 0, dtype=jnp.float32)
    back_one = lax.dot_general(mid_slope, w_mid, contract_cols, preferred_element_type=jnp.float32)
    in_slope = (back_one * silu_slope(pre_one)).astype(jnp.bfloat16)
    in_grad = lax.dot_general(
        row_block, in_slope, contract_rows, preferred_element_type=jnp.float32
    )
    in_bias = jnp.sum(in_slope, 0, dtype=jnp.float32)
    row_grad = lax.dot_general(
        in_slope, w_in, contract_cols, preferred_element_type=jnp.float32
    ).astype(jnp.bfloat16)
    in_grad, in_bias, mid_grad, mid_bias, out_grad = lax.psum(
        (in_grad, in_bias, mid_grad, mid_bias, out_grad), ("graph", "leaf")
    )
    return (row_grad, (in_grad, in_bias, mid_grad, mid_bias, out_grad))


def body(
    features,
    positions,
    energy_weight,
    send_slot,
    tile_slot,
    box_count,
    list_box,
    list_image,
    w_in,
    b_in,
    w_mid,
    b_mid,
    w_out,
):
    box_dev = box_count.shape[0]
    tile_rows = box_dev * SLOT_DEV
    box_total = box_dev * lax.axis_size("leaf")
    atom_dev = send_slot.shape[0]
    atom_order = jnp.arange(atom_dev, dtype=jnp.int32)
    inverse_send = jnp.zeros((atom_dev,), jnp.int32).at[send_slot].set(atom_order)
    tile_source = jnp.full((tile_rows,), atom_dev, jnp.int32).at[tile_slot].set(atom_order)
    occupied = (tile_source < atom_dev).astype(jnp.float32)
    in_box = (jnp.arange(tile_rows, dtype=jnp.int32) % SLOT_DEV).reshape(
        box_dev, SLOT_DEV
    ) < box_count
    live_mask = in_box.reshape(tile_rows).astype(jnp.float32) * occupied
    pre_one, act_one, pre_two, act_two, atom_charge = head_forward(
        features, w_in, b_in, w_mid, b_mid, w_out
    )
    payload = jnp.concatenate(
        [positions, energy_weight[None], atom_charge[None], jnp.zeros((3, atom_dev), jnp.float32)],
        0,
    )
    outgoing = payload.T[inverse_send]
    incoming = lax.all_to_all(outgoing, ("graph", "leaf"), split_axis=0, concat_axis=0, tiled=True)
    padded_rows = jnp.concatenate([incoming, jnp.zeros((1, incoming.shape[1]), jnp.float32)], 0)
    placed = padded_rows[tile_source].T
    tile_charge = placed[4]
    charge = tile_charge * live_mask
    offsets_t = placed[:3]
    weighted = 0.5 * coupling * placed[3] * charge
    ones_pos = jnp.concatenate([jnp.ones((1, tile_rows), jnp.float32), offsets_t], 0)
    moments = jnp.sum((charge * ones_pos).reshape(4, box_dev, SLOT_DEV), -1)
    local_bar = jnp.sum((weighted * ones_pos).reshape(4, box_dev, SLOT_DEV), -1)
    first_box = lax.axis_index("leaf") * box_dev
    own_boxes = first_box + jnp.arange(box_dev, dtype=jnp.int32)
    moments, local_bar = lax.psum((moments, local_bar), "graph")
    all_moments = lax.all_gather(moments, "leaf", axis=1, tiled=True)
    grid_dims = jnp.array([8.0, 8.0, box_total // 64], jnp.float32).reshape(3, 1, 1)
    separation = (
        box_coords(list_box)
        + list_image.astype(jnp.float32) * grid_dims
        - box_coords(own_boxes)[:, :, None]
    )
    local_exp = jnp.sum(translate(separation, all_moments[:, list_box]), -1)
    back_terms = translate_back(separation, local_bar)
    spread_bar = jnp.zeros((4, box_total), jnp.float32).at[:, list_box].add(back_terms)
    moment_bar = lax.psum_scatter(spread_bar, "leaf", scatter_dimension=1, tiled=True)
    shaped = offsets_t.reshape(3, box_dev, SLOT_DEV)
    potential = local_exp[0][:, None] + jnp.sum(local_exp[1:, :, None] * shaped, 0)
    weight_tile = placed[3].reshape(box_dev, SLOT_DEV)
    grad_q = (
        (
            0.5 * coupling * weight_tile * potential
            + moment_bar[0][:, None]
            + jnp.sum(moment_bar[1:, :, None] * shaped, 0)
        )
        * live_mask.reshape(box_dev, SLOT_DEV)
    ).reshape(tile_rows)
    pos_tile = (
        weighted.reshape(box_dev, SLOT_DEV)[None] * local_exp[1:, :, None]
        + charge.reshape(box_dev, SLOT_DEV)[None] * moment_bar[1:, :, None]
    ).reshape(3, tile_rows)
    back_payload = jnp.concatenate([pos_tile, grad_q[None]], 0)
    leaving_rows = back_payload.T[tile_slot]
    arrived_back = lax.all_to_all(
        leaving_rows, ("graph", "leaf"), split_axis=0, concat_axis=0, tiled=True
    )
    returned_rows = arrived_back[send_slot]
    position_grad = returned_rows[:, :3].T
    feature_grad, weight_grads = head_backward(
        features,
        pre_one,
        act_one,
        pre_two,
        act_two,
        returned_rows[:, 3].astype(jnp.bfloat16),
        w_in,
        w_mid,
        w_out,
    )
    in_grad, in_bias, mid_grad, mid_bias, out_grad = weight_grads
    return (feature_grad, position_grad, in_grad, in_bias, mid_grad, mid_bias, out_grad)


def solution(mesh):
    placed = (
        P(("graph", "leaf"), None),
        P(None, ("graph", "leaf")),
        P(("graph", "leaf")),
        P(("graph", "leaf")),
        P(("graph", "leaf")),
        P("leaf", "graph"),
        P("leaf", None),
        P(None, "leaf", None),
        P(),
        P(),
        P(),
        P(),
        P(),
    )
    return jax.shard_map(
        body,
        mesh=mesh,
        in_specs=placed,
        out_specs=(P(("graph", "leaf"), None), P(None, ("graph", "leaf")), P(), P(), P(), P(), P()),
        check_vma=False,
    )
```

profile of v0, /device:TPU:1, one launch (start us, length us, event | category | flops | bytes accessed | tf_op | source)
XLA Modules:
  0.0 695.1 jit_solution(3503960751309952907)
XLA Ops:
  7.9 7.8 %multiply_convert_fusion.2 = (bf16[8192,256]{1,0:T(8,128)(2,1)S(1)}, f32[8192,256]{1,0:T(8,128)}) fusion(f32[256]{0:T(256)} %param.23, bf16[8192,256]{1,0:T(8,128)(2,1)} %param.14, bf16[256,256]{1,0:T(8,128)(2,1)} %param.22), kind=kOutput, calls=%fused_computation.19 | convolution fusion | flops 1086324736 | bytes 16909312 | tf_op jit(solution)/shard_map/dot_general | solution.py:52
  15.7 4.5 multiply_convert_fusion.1
  26.2 30.5 %scatter_custom_fusion = s32[8192]{0:T(1024)S(1)} fusion(s32[8192]{0:T(1024)S(1)} %get-tuple-element.84, s32[8192]{0:T(1024)S(1)} %iota.15, s32[]{:T(128)} %constant.106.clone.1), kind=kCustom, calls=%fused_computation.104 | custom fusion | bytes 32772 | tf_op jit(solution)/shard_map/scatter | solution.py:106
  56.7 29.9 %gather_fusion = f32[8192,8]{1,0:T(8,128)} fusion(f32[8192,8]{1,0:T(8,128)} %bitcast.107, s32[8192]{0:T(1024)S(1)} %fusion.19), kind=kCustom, calls=%fused_computation | custom fusion | bytes 557056 | tf_op jit(solution)/shard_map/gather | solution.py:120
  90.4 11.5 %all-to-all-start = ((f32[128,1,512]{2,1,0:T(1,128)}), f32[128,1,512]{2,1,0:T(1,128)S(1)}, u32[]{:S(2)}, u32[]{:S(2)}) async-start(f32[128,1,512]{2,1,0:T(1,128)} %reshape.409), calls=%async_computation | async-start | bytes 524288 | tf_op jit(solution)/shard_map/all_to_all | solution.py:121
  102.1 30.7 %scatter_custom_fusion.1 = s32[16384]{0:T(1024)S(1)} fusion(s32[8192]{0:T(1024)S(1)} %get-tuple-element.86, s32[8192]{0:T(1024)S(1)} %iota.16, s32[]{:T(128)} %constant.107.clone.1), kind=kCustom, calls=%fused_computation.94 | custom fusion | bytes 65540 | tf_op jit(solution)/shard_map/scatter | solution.py:107
  137.7 3.8 concatenate.23
  141.5 56.6 %gather_fusion.1 = f32[16384,8]{1,0:T(8,128)} fusion(f32[8193,8]{1,0:T(8,128)} %concatenate.23, s32[16384]{0:T(1024)S(1)} %fusion.10), kind=kCustom, calls=%fused_computation.1 | custom fusion | bytes 1114112 | tf_op jit(solution)/shard_map/gather | solution.py:123
  198.0 5.6 copy.120
  204.0 5.1 copy.134
  209.2 4.9 bitcast_reduce_fusion
  214.3 24.8 %all-reduce.4 = (f32[4,128]{0,1:T(8,128)S(1)}, f32[4,128]{0,1:T(8,128)S(1)}) all-reduce(f32[4,128]{0,1:T(8,128)S(1)} %copy.121, f32[4,128]{0,1:T(8,128)S(1)} %bitcast_reduce_fusion), channel_id=1, replica_groups=mesh['graph'=8,'leaf'=16] {'graph'}, use_global_device_ids=true, to_apply=%region_3.4 | all-reduce | flops 1024 | bytes 8192 | tf_op jit(solution)/shard_map/psum | solution.py:133
  239.3 20.1 %all_gather.3 = f32[4,2048]{0,1:T(8,128)S(1)} all-gather(f32[4,128]{0,1:T(8,128)S(1)} %get-tuple-element.66), channel_id=1, replica_groups=mesh['graph'=8,'leaf'=16] {'leaf'}, dimensions={1}, use_global_device_ids=true | all-gather | bytes 34816 | tf_op jit(solution)/shard_map/all_gather | solution.py:134
  259.4 28.0 %gather_fusion.2 = f32[8192,4]{1,0:T(8,128)} fusion(f32[4,2048]{0,1:T(8,128)S(1)} %all_gather.3, s32[8192]{0:T(1024)S(1)} %broadcast_clamp_fusion.1), kind=kCustom, calls=%fused_computation.2 | custom fusion | bytes 294912 | tf_op jit(solution)/shard_map/gather | solution.py:141
  287.4 3.7 copy.123
  291.5 4.4 copy.135
  295.9 45.4 %scatter_custom_fusion.2 = f32[4,2048]{0,1:T(8,128)} fusion(s32[8192]{0:T(1024)S(1)} %reshape.338, f32[8192,4]{1,0:T(8,128)} %bitcast.113, f32[]{:T(128)} %constant.105.clone.1), kind=kCustom, calls=%fused_computation.25 | custom fusion | flops 32768 | bytes 33280 | tf_op jit(solution)/shard_map/scatter-add | solution.py:143
  341.5 75.7 %reduce-scatter.2.cloned.1.call-done = f32[4,128]{0,1:T(8,128)} async-done(((f32[4,2048]{0,1:T(8,128)}), f32[4,128]{0,1:T(8,128)}) %reduce-scatter.2.cloned.1.call-update) | async-done | bytes 2064 | tf_op jit(solution)/shard_map/reduce_scatter | solution.py:144
  420.4 5.1 copy.129
  425.5 31.3 %gather_fusion.3 = f32[8192,4]{1,0:T(8,128)} fusion(f32[16384,4]{1,0:T(8,128)} %copy.129, s32[8192]{0:T(1024)S(1)} %get-tuple-element.85), kind=kCustom, calls=%fused_computation.3 | custom fusion | bytes 294912 | tf_op jit(solution)/shard_map/gather | solution.py:161
  456.8 3.0 copy.130
  460.8 9.3 %all-to-all-start.1 = ((f32[128,1,256]{2,1,0:T(1,128)}), f32[128,1,256]{2,1,0:T(1,128)S(1)}, u32[]{:S(2)}, u32[]{:S(2)}) async-start(f32[128,1,256]{2,1,0:T(1,128)} %reshape.411), calls=%async_computation.2 | async-start | bytes 262144 | tf_op jit(solution)/shard_map/all_to_all | solution.py:162
  470.3 9.8 %all-to-all-done.1 = f32[128,1,256]{2,1,0:T(1,128)S(1)} async-done(((f32[128,1,256]{2,1,0:T(1,128)}), f32[128,1,256]{2,1,0:T(1,128)S(1)}, u32[]{:S(2)}, u32[]{:S(2)}) %all-to-all-start.1) | async-done | bytes 131104 | tf_op jit(solution)/shard_map/all_to_all | solution.py:162
  484.0 29.9 %gather_fusion.4 = f32[8192,4]{1,0:T(8,128)} fusion(f32[8192,4]{1,0:T(8,128)} %bitcast.108, s32[8192]{0:T(1024)S(1)} %get-tuple-element.83), kind=kCustom, calls=%fused_computation.4 | custom fusion | bytes 294912 | tf_op jit(solution)/shard_map/gather | solution.py:165
  513.9 3.9 fusion.1
  517.8 4.6 slice_bitcast_fusion
  523.1 6.7 convert_reduce_fusion
  532.0 3.6 convert_reduce_fusion.1
  539.6 3.5 copy.132
  543.1 62.7 %all-reduce.2 = (f32[256]{0:T(256)}, f32[256]{0:T(256)}, f32[256]{0:T(256)}) all-reduce(f32[256]{0:T(256)S(1)} %get-tuple-element.96, f32[256]{0:T(256)S(1)} %get-tuple-element.68, f32[256]{0:T(256)S(1)} %bitcast.133), channel_id=1, replica_groups=mesh['graph'=8,'leaf'=16] {'graph','leaf'}, use_global_device_ids=true, to_apply=%region_16.17 | all-reduce | flops 768 | bytes 6144 | tf_op jit(solution)/shard_map/psum | solution.py:80
  605.8 5.5 convolution_convert_fusion
  611.3 73.5 %all-reduce.7.cloned.1.call-done = (f32[256,256]{0,1:T(8,128)}, f32[256,256]{1,0:T(8,128)}) async-done(((f32[256,256]{0,1:T(8,128)}, f32[256,256]{1,0:T(8,128)}), (f32[256,256]{0,1:T(8,128)}, f32[256,256]{1,0:T(8,128)})) %all-reduce.7.cloned.1.call-update) | async-done | bytes 524304 | tf_op jit(solution)/shard_map/psum | solution.py:80
  (113 shorter events, 35.3 us)
Async XLA Ops:
  7.2 8.5 %copy-start = (bf16[256,256]{1,0:T(8,128)(2,1)S(1)}, bf16[256,256]{1,0:T(8,128)(2,1)}, u32[]{:S(2)}) copy-start(bf16[256,256]{1,0:T(8,128)(2,1)} %param.24) | copy-start | bytes 393220
  7.9 7.8 %copy-start.16 = (f32[256]{0:T(256)S(1)}, f32[256]{0:T(256)}, u32[]{:S(2)}) copy-start(f32[256]{0:T(256)} %param.25) | copy-start | bytes 3076
  15.7 4.5 copy-start.5
  20.1 2.0 copy-start.2
  20.1 3.2 copy-start.8
  20.1 3.2 copy-start.10
  22.1 4.0 copy-start.11
  86.6 15.4 %copy-start.12 = (s32[8192]{0:T(1024)S(1)}, s32[8192]{0:T(1024)}, u32[]{:S(2)}) copy-start(s32[8192]{0:T(1024)} %param.18) | copy-start | bytes 98308
  86.6 46.2 %copy-start.13 = (s32[128,64]{0,1:T(8,128)S(1)}, s32[128,64]{0,1:T(8,128)}, u32[]{:S(2)}) copy-start(s32[128,64]{0,1:T(8,128)} %param.20) | copy-start | bytes 98308
  90.4 42.6 %all-to-all-start = ((f32[128,1,512]{2,1,0:T(1,128)}), f32[128,1,512]{2,1,0:T(1,128)S(1)}, u32[]{:S(2)}, u32[]{:S(2)}) async-start(f32[128,1,512]{2,1,0:T(1,128)} %reshape.409), calls=%async_computation | async-start | bytes 524288 | tf_op jit(solution)/shard_map/all_to_all | solution.py:121
  101.9 315.2 %reduce-scatter.2.cloned.1.call-start = ((), (), s32[]{:S(2)}) async-start(), calls=%async_computation.3 | async-start | bytes 1114112 | tf_op jit(solution)/shard_map/reduce_scatter | solution.py:144
  198.0 5.7 copy-start.14
  214.2 77.0 %copy-start.9 = (s32[3,128,64]{1,2,0:T(8,128)S(1)}, s32[3,128,64]{1,2,0:T(8,128)}, u32[]{:S(2)}) copy-start(s32[3,128,64]{1,2,0:T(8,128)} %param.21) | copy-start | bytes 294916
  214.2 77.0 %copy-start.15 = (f32[3]{0:T(128)S(1)}, f32[3]{0:T(128)}, u32[]{:S(2)}) copy-start(f32[3]{0:T(128)} %constant.123.clone) | copy-start | bytes 40
  456.8 13.5 %copy-start.17 = (bf16[256]{0:T(256)(128)(2,1)S(1)}, bf16[256]{0:T(256)(128)(2,1)}, u32[]{:S(2)}) copy-start(bf16[256]{0:T(256)(128)(2,1)} %param.26) | copy-start | bytes 1540
  460.8 19.3 %all-to-all-start.1 = ((f32[128,1,256]{2,1,0:T(1,128)}), f32[128,1,256]{2,1,0:T(1,128)S(1)}, u32[]{:S(2)}, u32[]{:S(2)}) async-start(f32[128,1,256]{2,1,0:T(1,128)} %reshape.411), calls=%async_computation.2 | async-start | bytes 262144 | tf_op jit(solution)/shard_map/all_to_all | solution.py:162
  470.0 214.8 %all-reduce.7.cloned.1.call-start = ((), (), s32[]{:S(2)}) async-start(), calls=%async_computation.4 | async-start | bytes 1048576 | tf_op jit(solution)/shard_map/psum | solution.py:80
  517.8 4.6 copy-start.3
  523.1 6.7 copy-start.6
  523.1 8.8 %slice-start = ((s8[8388608]{0:T(1024)(128)(4,1)}), s8[4194304]{0:T(1024)(128)(4,1)S(1)}, s32[]{:S(2)}) async-start(s8[8388608]{0:T(1024)(128)(4,1)} %bitcast.135), calls=%async_computation.5 | async-start | bytes 8388608
  529.8 2.2 slice-start.1
  532.0 5.6 copy-start.4
  535.7 1.9 copy-start.1
  539.6 66.2 %copy-start.7 = (bf16[256,256]{1,0:T(8,128)(2,1)S(1)}, bf16[256,256]{1,0:T(8,128)(2,1)}, u32[]{:S(2)}) copy-start(bf16[256,256]{1,0:T(8,128)(2,1)} %param.22) | copy-start | bytes 393220
Sparse Core Ops, SparseCore 0:
  341.4 75.6 reduce-scatter.1
  543.2 141.5 all-reduce.6
where the time goes:
time: 696 us; the launch traced here: 695 us
  local copies, waits for them, and re-layouts  305 us (44%)
  waiting for transfers between devices  159 us (23%)
  blocking collectives  108 us (16%)
  other arithmetic  61.2 us (9%)
  matrix products  27.2 us (4%)
  starting transfers between devices  21.1 us (3%)
  between operations  14.5 us (2%)
    reduce_scatter x1, waiting for transfers between devices, body(): lax.psum_scatter(spread_bar, 'leaf', scatter_dimension=1, tiled=True)  75.7 us
    psum x1, waiting for transfers between devices, head_backward(): lax.psum((in_grad, in_bias, mid_grad, mid_bias, out_grad), ('graph', 'lea...  73.5 us
    psum x1, blocking collectives, head_backward(): lax.psum((in_grad, in_bias, mid_grad, mid_bias, out_grad), ('graph', 'lea...  62.7 us
    gather x2, local copies, waits for them, and re-layouts, body(): placed = padded_rows[tile_source].T  62.1 us
    scatter-add x1, other arithmetic, body(): jnp.zeros((4, box_total), jnp.float32).at[:, list_box].add(back_terms)  45.4 us
    gather x2, local copies, waits for them, and re-layouts, body(): local_exp = jnp.sum(translate(separation, all_moments[:, list_box]), -1)  31.7 us
    gather x1, local copies, waits for them, and re-layouts, body(): leaving_rows = back_payload.T[tile_slot]  31.3 us
    scatter x1, local copies, waits for them, and re-layouts, body(): jnp.full((tile_rows,), atom_dev, jnp.int32).at[tile_slot].set(atom_order)  30.7 us
  transfers between devices with their start and end apart: 4, of which 3 were waited for; matrix products, arithmetic and copies ran while one was open for 5% of the time, Pallas kernels for 0%

commit v1 on v0

v1 whole, which is shorter than its diff:
```python
import functools

import jax
import jax.numpy as jnp
from jax import lax
from jax.experimental import pallas as pl
from jax.experimental.pallas import tpu as pltpu
from jax.sharding import PartitionSpec as P

MESH = pl.DeviceIdType.MESH
F32 = jnp.float32
BF16 = jnp.bfloat16
COUPLING = 0.5
SLOT_DEV = 128
NT = (((1,), (1,)), ((), ()))
NN = (((1,), (0,)), ((), ()))
TN = (((0,), (0,)), ((), ()))


def mm(a, b, dims=NN):
    return lax.dot_general(a, b, dims, preferred_element_type=F32)


def iota(shape, axis):
    return lax.broadcasted_iota(jnp.int32, shape, axis)


def tile_lanes(x, n):
    return jnp.concatenate([x] * (n // x.shape[1]), 1)


def fold_lanes(x):
    parts = [x[:, i : i + 128] for i in range(0, x.shape[1], 128)]
    total = parts[0]
    for part in parts[1:]:
        total = total + part
    return total


def roll(x, shift):
    return pltpu.roll(x, shift % 128, 1)


def shift_x(x):
    first = roll(pltpu.roll(x, 120, 1, stride=1, stride_axis=0), 6)
    col = iota(x.shape, 1) % 8 + 2 - iota(x.shape, 0)
    return jnp.where(col > 7, roll(first, 8), jnp.where(col < 0, roll(first, -8), first))


def shift_y(x, dy):
    if dy == 0:
        return x
    straight = roll(x, -8 * dy)
    row = (iota(x.shape, 1) // 8) % 8 + dy
    return jnp.where((row >= 0) & (row < 8), straight, roll(straight, 64))


def shift_z(slabs, dz):
    if dz % 2 == 0:
        return slabs[dz // 2 + 1]
    low, high = (0, 1) if dz == -1 else (1, 2)
    lower = iota(slabs[0].shape, 1) < 64
    return jnp.where(lower, roll(slabs[low], 64), roll(slabs[high], 64))


def kernel(
    n_graph, n_leaf, chunk, n_grp,
    feat, pos, ew, sslot, tslot, count, lbox, limg, w_in, b_in, w_mid, b_mid, w_out,
    fgrad, pgrad, ing, inb, midg, midb, outg,
    X, A1, SL1, A2, SL2, OB, U, Q, W1H, W1T, W2TH, W2H, B1, B2, WO, WOH,
    CODE, CA, CB, CS, F, G, GN, R, LCODE, MX, P1, S1, P2, TO, TB,
    MIDACC, INACC, OGACC, IBACC, MIDS, INS, RM, RI, GS, GM, AS, AM, BV, BL, BS, BG,
    xsem, osem, ssem, rsem,
):
    g = lax.axis_index("graph")
    l = lax.axis_index("leaf")
    atoms = X.shape[0]
    hid = SL1.shape[0]
    cap = atoms // (n_graph * n_leaf)
    leaf_bits = n_leaf.bit_length() - 1
    cap_bits = cap.bit_length() - 1
    code_rows = n_leaf * cap // 128
    box_dev = 128
    wrow = hid // n_leaf

    def leaf_peer(o):
        return lax.rem(l + o, n_leaf)

    def graph_peer(o):
        return lax.rem(g + o, n_graph)

    def to_leaf(k, src_of, dst):
        @pl.loop(1, n_leaf)
        def _(o):
            peer = leaf_peer(o)
            pltpu.make_async_remote_copy(
                src_ref=src_of(peer), dst_ref=dst, send_sem=ssem.at[k], recv_sem=rsem.at[k],
                device_id=(g, peer), device_id_type=MESH,
            ).start()

    def to_graph(k, src_of, dst):
        @pl.loop(1, n_graph)
        def _(o):
            peer = graph_peer(o)
            pltpu.make_async_remote_copy(
                src_ref=src_of(peer), dst_ref=dst, send_sem=ssem.at[k], recv_sem=rsem.at[k],
                device_id=(peer, l), device_id_type=MESH,
            ).start()

    def wait_on(sem, view):
        pltpu.make_async_copy(view, view, sem).wait()

    bar = pltpu.get_barrier_semaphore()

    @pl.loop(1, n_leaf)
    def _(o):
        pl.semaphore_signal(bar, inc=1, device_id=(g, leaf_peer(o)), device_id_type=MESH)

    @pl.loop(1, n_graph)
    def _(o):
        pl.semaphore_signal(bar, inc=1, device_id=(graph_peer(o), l), device_id_type=MESH)

    n_chunks = atoms // chunk

    def feat_copy(c):
        rows = pl.ds(c * chunk, chunk)
        return pltpu.make_async_copy(feat.at[rows], X.at[rows], xsem.at[c])

    @pl.loop(0, n_chunks)
    def _(c):
        feat_copy(c).start()

    slot = tslot[...]
    box = slot >> 7

    def count_step(b, cnt):
        return jnp.where(box == b, count[b, 0], cnt)

    cnt = lax.fori_loop(0, box_dev, count_step, jnp.zeros_like(slot), unroll=8)
    CODE[...] = jnp.where((slot & (SLOT_DEV - 1)) < cnt, box, -1).astype(F32)

    pl.semaphore_wait(bar, n_leaf + n_graph - 2)
    CA[g] = CODE[pl.ds(pl.multiple_of(g * code_rows, code_rows), code_rows), :]
    to_graph(
        0,
        lambda peer: CODE.at[pl.ds(pl.multiple_of(peer * code_rows, code_rows), code_rows)],
        CA.at[g],
    )

    own = l * box_dev + iota((box_dev, lbox.shape[1]), 0)
    src = lbox[...]
    dims = (8, 8, n_leaf * box_dev // 64)
    dx, dy, dz = [
        coord(src) + limg[i] * dims[i] - coord(own)
        for i, coord in enumerate([lambda b: b & 7, lambda b: (b >> 3) & 7, lambda b: b >> 6])
    ]
    code = (((dz + 2) * 5 + dy + 2) * 8 + 2 - dx).astype(F32)
    code = jnp.concatenate([code, jnp.zeros((box_dev, 128 - code.shape[1]), F32)], 1)
    LCODE[...] = code.T.astype(jnp.int32)
    F[...] = jnp.zeros_like(F)
    sub = iota((8, 128), 0)

    def mask_step(k, masks):
        row = LCODE[pl.ds(k, 1), :] - sub
        return tuple(m + jnp.where(row == 8 * i, 1.0, 0.0) for i, m in enumerate(masks))

    masks = lax.fori_loop(
        0, lbox.shape[1], mask_step, tuple(jnp.zeros((8, 128), F32) for _ in range(n_grp)), unroll=4
    )
    G[...] = jnp.zeros_like(G)
    for i in range(n_grp):
        F[8 * i : 8 * i + 8, :] = masks[i]
    for i in range(n_grp):
        for j in range(5):
            other = 8 * (n_grp - 1 - i) + 4 - j
            G[8 * i + j : 8 * i + j + 1, :] = F[other : other + 1, :]
    for k, step in ((2, 1), (3, n_leaf - 1)):
        pltpu.make_async_remote_copy(
            src_ref=G, dst_ref=GN.at[k - 2], send_sem=ssem.at[k], recv_sem=rsem.at[k],
            device_id=(g, leaf_peer(step)), device_id_type=MESH,
        ).start()

    w1 = w_in[...].astype(F32).T
    W1T[...] = w1.astype(BF16)
    W1H[...] = (0.5 * w1).astype(BF16)
    w2 = w_mid[...].astype(F32)
    W2H[...] = (0.5 * w2).astype(BF16)
    W2TH[...] = (0.5 * w2.T).astype(BF16)

    def column(row):
        return jnp.broadcast_to(row, (128, hid)).T

    B1[...] = column(0.5 * b_in[...])
    B2[...] = column(0.5 * b_mid[...])
    wo = column(w_out[...].astype(F32))
    WO[...] = wo
    WOH[...] = 0.5 * wo
    A1[hid:, :] = jnp.ones((A1.shape[0] - hid, atoms), BF16)
    U[...] = jnp.ones_like(U)
    U[1:4, :] = pos[...]
    U[5:8, :] = pos[...]

    def head(c):
        feat_copy(c).wait()
        cols = pl.ds(pl.multiple_of(c * chunk, chunk), chunk)
        h = mm(W1H[...], X[pl.ds(pl.multiple_of(c * chunk, chunk), chunk), :], NT)
        h = h + tile_lanes(B1[...], chunk)
        t = jnp.tanh(h)
        p = h * t
        a = (h + p).astype(BF16)
        A1[:hid, cols] = a
        SL1[:, cols] = ((1.0 + t) * (1.0 + (h - p))).astype(BF16)
        h = mm(W2TH[...], a) + tile_lanes(B2[...], chunk)
        t = jnp.tanh(h)
        p = h * t
        a = h + p
        A2[:, cols] = a.astype(BF16)
        SL2[:, cols] = (
            tile_lanes(WOH[...], chunk) * ((1.0 + t) * (1.0 + (h - p)))
        ).astype(BF16)
        Q[:, cols] = jnp.sum(a * tile_lanes(WO[...], chunk), 0, keepdims=True)

    first = n_chunks // 2
    pl.loop(0, first)(head)

    wait_on(rsem.at[0], CA.at[pl.ds(0, n_graph - 1)])
    flat = CA[...]
    for r in range(code_rows):
        CB[r] = flat[:, r, :]
    half = 128 // cap
    CS[l] = CB[l // half]
    to_leaf(1, lambda peer: CB.at[peer // half], CS.at[l])

    wait_on(rsem.at[2], GN.at[0])
    wait_on(rsem.at[3], GN.at[1])
    for i in range(n_grp):
        at = pl.ds(8 * i, 8)
        slabs = [shift_x(x) for x in (GN[0, at, :], G[at, :], GN[1, at, :])]
        R[at, :] = shift_y(shift_z(slabs, i // 5 - 2), i % 5 - 2)

    pl.loop(first, n_chunks)(head)

    wait_on(rsem.at[1], CS.at[pl.ds(0, n_leaf - 1)])
    codes = CS[...].reshape(n_leaf * n_graph, 128).T
    mine = codes[:cap]
    for i in range(1, half):
        mine = jnp.where(lax.rem(l, half) == i, codes[i * cap : (i + 1) * cap], mine)
    mine = mine.astype(BF16)
    MIDACC[...] = jnp.zeros_like(MIDACC)
    macc = MIDACC.at[pl.ds(0, 2 * n_leaf * 8), pl.ds(0, 128)]

    def scale_row(cols):
        return (0.5 * COUPLING) * ew[:, cols]

    def one_hot(index, n):
        return jnp.where(iota((n, chunk), 0) == index, 1.0, 0.0).astype(BF16)

    def place(c):
        cols = pl.ds(pl.multiple_of(c * chunk, chunk), chunk)
        s = sslot[:, cols]
        src_leaf = (s >> cap_bits) & (n_leaf - 1)
        row = src_leaf * n_graph + (s >> (cap_bits + leaf_bits))
        picked = mm(mine, one_hot(row, n_leaf * n_graph))
        in_row = iota((cap, chunk), 0) == (s & (cap - 1))
        atom_box = jnp.sum(jnp.where(in_row, picked, 0.0), 0, keepdims=True)
        ob = one_hot(atom_box.astype(jnp.int32), box_dev)
        OB[:, cols] = ob
        q = Q[:, cols]
        sub = iota((8, chunk), 0)
        vals = U[:, cols] * jnp.where(sub < 4, q, scale_row(cols) * q)
        hi = vals.astype(BF16).astype(F32)
        lo = vals - hi
        blocks = [jnp.where(src_leaf == i, hi, 0.0) for i in range(n_leaf)]
        blocks += [jnp.where(src_leaf == i, lo, 0.0) for i in range(n_leaf)]
        macc[...] += mm(jnp.concatenate(blocks, 0).astype(BF16), ob, NT)

    pl.loop(0, n_chunks)(place)

    rows = n_leaf * 8
    part = macc[:rows, :] + macc[rows:, :]
    MX[8 : rows + 8, :] = part
    MX[:8, :] = part[rows - 8 :]
    MX[rows + 8 :, :] = part[:8]
    P1[l] = MX[pl.ds(pl.multiple_of(l * 8, 8), 24), :]
    to_leaf(4, lambda peer: MX.at[pl.ds(pl.multiple_of(peer * 8, 8), 24)], P1.at[l])
    wait_on(rsem.at[4], P1.at[pl.ds(0, n_leaf - 1)])
    total = jnp.sum(P1[...], 0)
    S1[...] = total
    P2[g] = total
    to_graph(5, lambda peer: S1, P2.at[g])
    wait_on(rsem.at[5], P2.at[pl.ds(0, n_graph - 1)])
    total = jnp.sum(P2[...], 0)

    shifted = []
    for ch in range(8):
        slabs = [
            shift_x(jnp.broadcast_to(total[8 * s + ch : 8 * s + ch + 1], (8, 128))) for s in range(3)
        ]
        shifted.append([shift_z(slabs, d) for d in range(-2, 3)])
    off_x = (2 - iota((8, 128), 0)).astype(F32)
    sums = [jnp.zeros((8, 128), F32) for _ in range(8)]
    for i in range(n_grp):
        off_z, off_y = i // 5 - 2, i % 5 - 2
        dist = jnp.maximum(off_x * off_x + float(off_z * off_z + off_y * off_y), 1.0)
        inv = lax.rsqrt(dist)
        cube = inv * inv * inv
        three = 3.0 * inv * inv
        for base, mask in ((0, F), (4, R)):
            m = mask[8 * i : 8 * i + 8, :]
            q0, q1, q2, q3 = [
                m * shift_y(shifted[base + j][off_z + 2], off_y) for j in range(4)
            ]
            proj = off_x * q1 + float(off_y) * q2 + float(off_z) * q3
            sums[base] += q0 * inv - proj * cube
            radial = q0 - three * proj
            sums[base + 1] += (radial * off_x + q1) * cube
            sums[base + 2] += (radial * float(off_y) + q2) * cube
            sums[base + 3] += (radial * float(off_z) + q3) * cube
    for j in range(8):
        TO[j : j + 1, :] = jnp.sum(sums[j], 0, keepdims=True)
    TB[l] = TO[...]
    to_leaf(6, lambda peer: TO, TB.at[l])
    wait_on(rsem.at[6], TB.at[pl.ds(0, n_leaf - 1)])
    table = TB[...].reshape(rows, 128)
    hi = table.astype(BF16)
    table = jnp.concatenate([hi, (table - hi.astype(F32)).astype(BF16)], 0)

    MIDACC[...] = jnp.zeros_like(MIDACC)
    INACC[...] = jnp.zeros_like(INACC)
    OGACC[...] = jnp.zeros_like(OGACC)
    IBACC[...] = jnp.zeros_like(IBACC)

    def backward_mid(c):
        cols = pl.ds(pl.multiple_of(c * chunk, chunk), chunk)
        src_leaf = (sslot[:, cols] >> cap_bits) & (n_leaf - 1)
        got = mm(table, OB[:, cols])
        got = got[:rows] + got[rows:]
        field = jnp.zeros((8, chunk), F32)
        for i in range(n_leaf):
            field += jnp.where(src_leaf == i, got[8 * i : 8 * i + 8], 0.0)
        sub = iota((8, chunk), 0)
        terms = field * U[:, cols]
        q = Q[:, cols]
        w = scale_row(cols)
        grad = jnp.sum(terms * jnp.where(sub < 4, w, 1.0), 0, keepdims=True)
        force = field * jnp.where(sub < 4, w * q, q)
        force = force + pltpu.roll(force, 4, 0)
        pgrad[:, cols] = force[1:4]
        grad = jnp.broadcast_to(grad, (16, chunk)).astype(BF16)
        ms = SL2[:, cols].reshape(hid // 16, 16, chunk) * grad[None]
        ms = ms.reshape(hid, chunk)
        SL2[:, cols] = ms
        MIDACC[...] += mm(A1[:, cols], ms, NT)
        og = A2[:, cols].reshape(hid // 16, 16, chunk) * grad[None]
        OGACC[...] += fold_lanes(og.reshape(hid, chunk).astype(F32))

    pl.loop(0, n_chunks)(backward_mid)

    def shares(src, sems, dst):
        dst[l] = src[pl.ds(pl.multiple_of(l * wrow, wrow), wrow), :]
        to_leaf(sems, lambda peer: src.at[pl.ds(pl.multiple_of(peer * wrow, wrow), wrow)], dst.at[l])

    MIDS[...] = MIDACC[:hid, :].astype(BF16)
    shares(MIDS, 7, RM)

    def backward_in(c):
        cols = pl.ds(pl.multiple_of(c * chunk, chunk), chunk)
        slope = mm(W2H[...], SL2[:, cols]) * SL1[:, cols].astype(F32)
        IBACC[...] += fold_lanes(slope)
        slope = slope.astype(BF16)
        SL1[:, cols] = slope
        INACC[...] += mm(slope, X[pl.ds(pl.multiple_of(c * chunk, chunk), chunk), :])

    pl.loop(0, n_chunks)(backward_in)
    INS[...] = INACC[...].astype(BF16)
    shares(INS, 8, RI)

    def to_row(columns):
        return jnp.sum(columns.T, 0, keepdims=True)

    BV[...] = jnp.zeros_like(BV)
    vectors = (MIDACC[hid : hid + 1, :], to_row(OGACC[...]), to_row(IBACC[...]))
    for i, vector in enumerate(vectors):
        for j in range(hid // 128):
            at = 2 * i + j
            BV[at : at + 1, :] = vector[:, 128 * j : 128 * j + 128]
    BL[l] = BV[...]
    to_leaf(9, lambda peer: BV, BL.at[l])

    def out_copy(c):
        rows = pl.ds(c * chunk, chunk)
        return pltpu.make_async_copy(X.at[rows], fgrad.at[rows], osem.at[c])

    def backward_row(c):
        at = pl.ds(pl.multiple_of(c * chunk, chunk), chunk)
        X[at, :] = mm(SL1[:, at], W1T[...], TN).astype(BF16)
        out_copy(c).start()

    cut = [n_chunks * i // 4 for i in range(5)]
    pl.loop(cut[0], cut[1])(backward_row)

    wait_on(rsem.at[7], RM.at[pl.ds(0, n_leaf - 1)])
    wait_on(rsem.at[8], RI.at[pl.ds(0, n_leaf - 1)])
    wait_on(rsem.at[9], BL.at[pl.ds(0, n_leaf - 1)])
    GS[:wrow, :] = jnp.sum(RM[...].astype(F32), 0).astype(BF16)
    GS[wrow:, :] = jnp.sum(RI[...].astype(F32), 0).astype(BF16)
    GM[g] = GS[...]
    BS[...] = jnp.sum(BL[...], 0)
    BG[g] = BS[...]
    to_graph(10, lambda peer: GS, GM.at[g])
    to_graph(11, lambda peer: BS, BG.at[g])
    pl.loop(cut[1], cut[2])(backward_row)
    wait_on(rsem.at[10], GM.at[pl.ds(0, n_graph - 1)])
    wait_on(rsem.at[11], BG.at[pl.ds(0, n_graph - 1)])
    AS[...] = jnp.sum(GM[...].astype(F32), 0).astype(BF16)
    AM[l] = AS[...]
    to_leaf(12, lambda peer: AS, AM.at[l])
    bias = jnp.sum(BG[...], 0)
    for i, out in enumerate((midb, outg, inb)):
        for j in range(hid // 128):
            out[:, 128 * j : 128 * j + 128] = bias[2 * i + j : 2 * i + j + 1]
    pl.loop(cut[2], cut[4])(backward_row)
    wait_on(rsem.at[12], AM.at[pl.ds(0, n_leaf - 1)])
    midg[...] = AM[:, :wrow, :].astype(F32).reshape(hid, hid)
    ing[...] = AM[:, wrow:, :].astype(F32).reshape(hid, hid).T

    wait_on(ssem.at[0], CA.at[pl.ds(0, n_graph - 1)])
    wait_on(ssem.at[1], CS.at[pl.ds(0, n_leaf - 1)])
    wait_on(ssem.at[2], GN.at[0])
    wait_on(ssem.at[3], GN.at[1])
    wait_on(ssem.at[4], P1.at[pl.ds(0, n_leaf - 1)])
    wait_on(ssem.at[5], P2.at[pl.ds(0, n_graph - 1)])
    wait_on(ssem.at[6], TB.at[pl.ds(0, n_leaf - 1)])
    wait_on(ssem.at[7], RM.at[pl.ds(0, n_leaf - 1)])
    wait_on(ssem.at[8], RI.at[pl.ds(0, n_leaf - 1)])
    wait_on(ssem.at[9], BL.at[pl.ds(0, n_leaf - 1)])
    wait_on(ssem.at[10], GM.at[pl.ds(0, n_graph - 1)])
    wait_on(ssem.at[11], BG.at[pl.ds(0, n_graph - 1)])
    wait_on(ssem.at[12], AM.at[pl.ds(0, n_leaf - 1)])

    @pl.loop(0, n_chunks)
    def _(c):
        out_copy(c).wait()


def body(
    features, positions, energy_weight, send_slot, tile_slot, box_count, list_box, list_image,
    w_in, b_in, w_mid, b_mid, w_out,
):
    n_graph, n_leaf = lax.axis_size("graph"), lax.axis_size("leaf")
    atoms, feat = features.shape
    hid = w_in.shape[1]
    chunk = min(512, atoms // 4)
    n_grp = 25
    code_rows = n_leaf * (atoms // (n_graph * n_leaf)) // 128
    wrow = hid // n_leaf
    vmem = pl.BlockSpec(memory_space=pltpu.VMEM)
    any_space = pl.BlockSpec(memory_space=pl.ANY)
    smem = pl.BlockSpec(memory_space=pltpu.SMEM)

    def v(shape, dtype=F32):
        return pltpu.VMEM(shape, dtype)

    scratch = [
        v((atoms, feat), BF16), v((hid + 16, atoms), BF16), v((hid, atoms), BF16),
        v((hid, atoms), BF16), v((hid, atoms), BF16), v((128, atoms), BF16),
        v((8, atoms)), v((1, atoms)),
        v((hid, feat), BF16), v((hid, feat), BF16), v((hid, hid), BF16), v((hid, hid), BF16),
        v((hid, 128)), v((hid, 128)), v((hid, 128)), v((hid, 128)),
        v((atoms // 128, 128)), v((n_graph, code_rows, 128)), v((code_rows, n_graph, 128)),
        v((n_leaf, n_graph, 128)),
        v((8 * n_grp, 128)), v((8 * n_grp, 128)), v((2, 8 * n_grp, 128)), v((8 * n_grp, 128)),
        v((128, 128), jnp.int32),
        v((n_leaf * 8 + 16, 128)), v((n_leaf, 24, 128)), v((24, 128)), v((n_graph, 24, 128)),
        v((8, 128)), v((n_leaf, 8, 128)),
        v((hid + 16, hid)), v((hid, feat)), v((hid, 128)), v((hid, 128)),
        v((hid, hid), BF16), v((hid, feat), BF16),
        v((n_leaf, wrow, hid), BF16), v((n_leaf, wrow, hid), BF16),
        v((2 * wrow, hid), BF16), v((n_graph, 2 * wrow, hid), BF16),
        v((2 * wrow, hid), BF16), v((n_leaf, 2 * wrow, hid), BF16),
        v((8, 128)), v((n_leaf, 8, 128)), v((8, 128)), v((n_graph, 8, 128)),
        pltpu.SemaphoreType.DMA((atoms // chunk,)), pltpu.SemaphoreType.DMA((atoms // chunk,)),
        pltpu.SemaphoreType.DMA((13,)), pltpu.SemaphoreType.DMA((13,)),
    ]
    sds = jax.ShapeDtypeStruct
    outs = pl.pallas_call(
        functools.partial(kernel, n_graph, n_leaf, chunk, n_grp),
        out_shape=(
            sds((atoms, feat), BF16), sds((3, atoms), F32),
            sds((feat, hid), F32), sds((1, hid), F32),
            sds((hid, hid), F32), sds((1, hid), F32), sds((1, hid), F32),
        ),
        in_specs=[any_space, vmem, vmem, vmem, vmem, smem] + [vmem] * 7,
        out_specs=(any_space,) + (vmem,) * 6,
        scratch_shapes=scratch,
        compiler_params=pltpu.CompilerParams(
            collective_id=0, has_side_effects=True, vmem_limit_bytes=60 * 1024 * 1024
        ),
        name="latent_charge",
    )(
        features, positions, energy_weight.reshape(1, atoms), send_slot.reshape(1, atoms),
        tile_slot.reshape(atoms // 128, 128), box_count, list_box, list_image,
        w_in, b_in.reshape(1, hid), w_mid, b_mid.reshape(1, hid), w_out.reshape(1, hid),
    )
    fgrad, pgrad, ing, inb, midg, midb, outg = outs
    return (fgrad, pgrad, ing, inb.reshape(hid), midg, midb.reshape(hid), outg.reshape(hid))


def solution(mesh):
    placed = (
        P(("graph", "leaf"), None),
        P(None, ("graph", "leaf")),
        P(("graph", "leaf")),
        P(("graph", "leaf")),
        P(("graph", "leaf")),
        P("leaf", "graph"),
        P("leaf", None),
        P(None, "leaf", None),
        P(), P(), P(), P(), P(),
    )
    return jax.shard_map(
        body,
        mesh=mesh,
        in_specs=placed,
        out_specs=(P(("graph", "leaf"), None), P(None, ("graph", "leaf")), P(), P(), P(), P(), P()),
        check_vma=False,
    )
```

time: 696 us -> 92.8 us (0.13)
  local copies, waits for them, and re-layouts: 305 us -> 14.1 us
  waiting for transfers between devices: 159 us -> 0 us
  blocking collectives: 108 us -> 0 us
  Pallas kernels: 0 us -> 77.7 us
  other arithmetic: 61.2 us -> 0 us
  matrix products: 27.2 us -> 0 us
  starting transfers between devices: 21.1 us -> 0 us
  between operations: 14.5 us -> 0.7 us
    gather x7 -> x0, local copies, waits for them, and re-layouts: 185 us -> none  [the longest x2 62.1 us: body(): placed = padded_rows[tile_source].T]
    psum x2 -> x0, blocking collectives: 87.5 us -> none  [the longest x1 62.7 us: head_backward(): lax.psum((in_grad, in_bias, mid_grad, mid_bias, out_grad), ('graph', 'lea...]
    pallas_call x0 -> x1, Pallas kernels: none -> 77.7 us  [body(): pl.pallas_call(functools.partial(kernel, n_graph, n_leaf, chunk, n_grp),...]
    reduce_scatter x1 -> x0, waiting for transfers between devices: 75.7 us -> none  [body(): lax.psum_scatter(spread_bar, 'leaf', scatter_dimension=1, tiled=True)]
    psum x1 -> x0, waiting for transfers between devices: 73.5 us -> none  [head_backward(): lax.psum((in_grad, in_bias, mid_grad, mid_bias, out_grad), ('graph', 'lea...]
    scatter x2 -> x0, local copies, waits for them, and re-layouts: 61.1 us -> none  [the longest x1 30.7 us: body(): jnp.full((tile_rows,), atom_dev, jnp.int32).at[tile_slot].set(atom_order)]
    scatter-add x1 -> x0, other arithmetic: 45.4 us -> none  [body(): jnp.zeros((4, box_total), jnp.float32).at[:, list_box].add(back_terms)]
    dot_general x8 -> x0, matrix products: 27.2 us -> none  [the longest x1 7.78 us: head_forward(): jnp.dot(row_block, w_in, preferred_element_type=jnp.float32) + b_in]
  transfers between devices with their start and end apart: 4 -> 0, of which waited for: 3 -> 0; matrix products, arithmetic and copies ran while one was open for 5% -> 0% of each run, Pallas kernels for 0% -> 0%
where the time goes in v1:
time: 92.8 us; the launch traced here: 92.4 us
  Pallas kernels  77.7 us (84%)
  local copies, waits for them, and re-layouts  14.1 us (15%)
    pallas_call x1, Pallas kernels, body(): pl.pallas_call(functools.partial(kernel, n_graph, n_leaf, chunk, n_grp),...  77.7 us
    unnamed x22, local copies, waits for them, and re-layouts  12.9 us

profile of v1, /device:TPU:1, one launch (start us, length us, event | category | flops | bytes accessed | tf_op | source)
XLA Modules:
  0.0 92.4 jit_solution(5818767897730166805)
XLA Ops:
  0.6 1.2 %reshape.46.w_out = bf16[1,256]{1,0:T(2,128)(2,1)} reshape(bf16[256]{0:T(256)(128)(2,1)} %param.25) | data formatting | bytes 1024 | tf_op jit(solution)/shard_map/reshape | solution.py:503
  1.9 1.4 %copy.20.count = s32[128,1]{1,0:T(8,128)} copy(s32[128,1]{0,1:T(1,128)} %param.18) | data formatting | bytes 1024 | tf_op args[5]
  3.2 1.5 %copy.21.lbox = s32[128,64]{1,0:T(8,128)} copy(s32[128,64]{0,1:T(8,128)} %param.19) | data formatting | bytes 65536 | tf_op args[6]
  4.7 1.7 %copy.22.limg = s32[3,128,64]{2,1,0:T(8,128)} copy(s32[3,128,64]{1,2,0:T(8,128)} %param.20) | data formatting | bytes 196608 | tf_op args[7]
  6.4 77.7 %latent_charge.1 = (bf16[8192,256]{1,0:T(8,128)(2,1)}, f32[3,8192]{1,0:T(4,128)}, f32[256,256]{1,0:T(8,128)}, f32[1,256]{1,0:T(1,128)}, f32[256,256]{1,0:T(8,128)}, /*index=5*/f32[1,256]{1,0:T(1,128)}, f32[1,256]{1,0:T(1,128)}) custom-call(bf16[8192,256]{1,0:T(8,128)(2,1)} %feat.1, f32[3,8192]{1,0:T(4,128)} %pos.1, f32[1,8192]{1,0:T(1,128)} %bitcast.8, ...), custom_call_target="tpu_custom_call" | custom-call | tf_op jit(solution)/shard_map/latent_charge/pallas_call | solution.py:486
  84.1 0.0 copy-start.2
  84.1 0.0 copy-start.1
  84.1 0.0 copy-start.5
  84.1 0.0 copy-start
  84.1 0.0 copy-start.4
  84.1 0.0 copy-start.3
  84.1 4.5 %copy.30 = bf16[8192,256]{1,0:T(8,128)(2,1)} copy(bf16[8192,256]{1,0:T(8,128)(2,1)} %get-tuple-element.28) | data formatting | bytes 8388608
  88.7 0.0 copy-done.2
  88.7 0.7 copy.31
  89.3 0.0 copy-done.1
  89.3 0.7 copy.32
  90.0 0.0 copy-done.5
  90.0 0.6 copy.33
  90.6 0.0 copy-done
  90.6 0.7 copy.34
  91.3 0.0 copy-done.4
  91.3 0.6 copy.35
  91.9 0.0 copy-done.3
  91.9 0.6 copy.36
Async XLA Ops:
  84.1 4.6 %copy-start.2 = (f32[3,8192]{1,0:T(4,128)S(1)}, f32[3,8192]{1,0:T(4,128)}, u32[]{:S(2)}) copy-start(f32[3,8192]{1,0:T(4,128)} %get-tuple-element.29) | copy-start | bytes 294916
  84.1 5.2 %copy-start.1 = (f32[256,256]{1,0:T(8,128)S(1)}, f32[256,256]{1,0:T(8,128)}, u32[]{:S(2)}) copy-start(f32[256,256]{1,0:T(8,128)} %get-tuple-element.30) | copy-start | bytes 786436
  84.1 5.9 %copy-start.5 = (f32[1,256]{1,0:T(1,128)S(1)}, f32[1,256]{1,0:T(1,128)}, u32[]{:S(2)}) copy-start(f32[1,256]{1,0:T(1,128)} %get-tuple-element.17) | copy-start | bytes 3076
  84.1 6.5 %copy-start = (f32[256,256]{1,0:T(8,128)S(1)}, f32[256,256]{1,0:T(8,128)}, u32[]{:S(2)}) copy-start(f32[256,256]{1,0:T(8,128)} %get-tuple-element.32) | copy-start | bytes 786436
  84.1 7.2 %copy-start.4 = (f32[1,256]{1,0:T(1,128)S(1)}, f32[1,256]{1,0:T(1,128)}, u32[]{:S(2)}) copy-start(f32[1,256]{1,0:T(1,128)} %get-tuple-element.19) | copy-start | bytes 3076
  84.1 7.7 %copy-start.3 = (f32[1,256]{1,0:T(1,128)S(1)}, f32[1,256]{1,0:T(1,128)}, u32[]{:S(2)}) copy-start(f32[1,256]{1,0:T(1,128)} %get-tuple-element.20) | copy-start | bytes 3076

commit v2 on v1

v2 whole, which is shorter than its diff:
```python
import functools

import jax
import jax.numpy as jnp
from jax import lax
from jax.experimental import pallas as pl
from jax.experimental.pallas import tpu as pltpu
from jax.sharding import PartitionSpec as P

MESH = pl.DeviceIdType.MESH
F32 = jnp.float32
BF16 = jnp.bfloat16
COUPLING = 0.5
SLOT_DEV = 128
CHUNK = 512
NT = (((1,), (1,)), ((), ()))
NN = (((1,), (0,)), ((), ()))
TN = (((0,), (0,)), ((), ()))


def mm(a, b, dims=NN):
    return lax.dot_general(a, b, dims, preferred_element_type=F32)


def iota(shape, axis):
    return lax.broadcasted_iota(jnp.int32, shape, axis)


def tile_lanes(x, n):
    return jnp.concatenate([x] * (n // x.shape[1]), 1)


def fold_lanes(x):
    parts = [x[:, i : i + 128] for i in range(0, x.shape[1], 128)]
    total = parts[0]
    for part in parts[1:]:
        total = total + part
    return total


def roll(x, shift):
    return pltpu.roll(x, shift % 128, 1)


def shift_x(x):
    first = roll(pltpu.roll(x, 120, 1, stride=1, stride_axis=0), 6)
    col = iota(x.shape, 1) % 8 + 2 - iota(x.shape, 0)
    return jnp.where(col > 7, roll(first, 8), jnp.where(col < 0, roll(first, -8), first))


def shift_y(x, dy):
    if dy == 0:
        return x
    straight = roll(x, -8 * dy)
    row = (iota(x.shape, 1) // 8) % 8 + dy
    return jnp.where((row >= 0) & (row < 8), straight, roll(straight, 64))


def shift_z(slabs, dz):
    if dz % 2 == 0:
        return slabs[dz // 2 + 1]
    low, high = (0, 1) if dz == -1 else (1, 2)
    lower = iota(slabs[1].shape, 1) < 64
    return jnp.where(lower, roll(slabs[low], 64), roll(slabs[high], 64))


def kernel(
    n_graph, n_leaf, chunk, n_grp,
    feat, pos, ew, sslot, tslot, count, lbox, limg, w_in, b_in, w_mid, b_mid, w_out,
    fgrad, pgrad, ing, inb, midg, midb, outg,
    X, A1, SL1, A2, SL2, OB, OD, BLK, U, Q, W1H, W1T, W2TH, W2H, B1, B2, WO,
    CODE, CA, CB, CS, F, G, GN, R, LCODE, MACC, MX, P1, S1, P2, TO, TB,
    ACC, OGACC, IBACC, BOTH, RX, SB, RM, GS, GM, AS, AM, AO,
    BV, BX, BC, BL, BS, BG,
    xsem, osem, ssem, rsem,
):
    g = lax.axis_index("graph")
    l = lax.axis_index("leaf")
    core = lax.rem(g, 2)
    zpos = g // 2
    atoms = X.shape[0]
    hid = SL1.shape[0]
    cap = atoms // (n_graph * n_leaf)
    leaf_bits = n_leaf.bit_length() - 1
    cap_bits = cap.bit_length() - 1
    code_rows = n_leaf * cap // 128
    box_dev = 128
    wrow = hid // n_leaf
    n_z = n_graph // 2
    n_chunks = atoms // chunk
    half_grp = 2 * (n_grp // 5)

    def leaf_peer(o):
        return lax.rem(l + o, n_leaf)

    def send(k, src, dst, device):
        pltpu.make_async_remote_copy(
            src_ref=src, dst_ref=dst, send_sem=ssem.at[k], recv_sem=rsem.at[k],
            device_id=device, device_id_type=MESH,
        ).start()

    def to_leaf(k, src_of, dst):
        @pl.loop(1, n_leaf)
        def _(o):
            peer = leaf_peer(o)
            send(k, src_of(peer), dst, (g, peer))

    def to_graph(k, src_of, dst):
        @pl.loop(1, n_graph)
        def _(o):
            peer = lax.rem(g + o, n_graph)
            send(k, src_of(peer), dst, (peer, l))

    def to_z(k, src, dst):
        @pl.loop(1, n_z)
        def _(o):
            send(k, src, dst, (lax.rem(g + 2 * o, n_graph), l))

    def to_core(k, src, dst):
        send(k, src, dst, (g + 1 - 2 * core, l))

    def wait_on(sem, view):
        pltpu.make_async_copy(view, view, sem).wait()

    bar = pltpu.get_barrier_semaphore()

    @pl.loop(1, n_leaf)
    def _(o):
        pl.semaphore_signal(bar, inc=1, device_id=(g, leaf_peer(o)), device_id_type=MESH)

    @pl.loop(1, n_graph)
    def _(o):
        pl.semaphore_signal(
            bar, inc=1, device_id=(lax.rem(g + o, n_graph), l), device_id_type=MESH
        )

    def feat_copy(c):
        rows = pl.ds(c * chunk, chunk)
        return pltpu.make_async_copy(feat.at[rows], X.at[rows], xsem.at[c])

    @pl.loop(0, n_chunks)
    def _(c):
        feat_copy(c).start()

    slot = tslot[...]
    box = slot >> 7

    def count_step(b, cnt):
        return jnp.where(box == b, count[0, b], cnt)

    cnt = lax.fori_loop(0, box_dev, count_step, jnp.zeros_like(slot), unroll=8)
    CODE[...] = jnp.where((slot & (SLOT_DEV - 1)) < cnt, box, -1).astype(F32)
    CA[g] = CODE[pl.ds(pl.multiple_of(g * code_rows, code_rows), code_rows), :]

    w1 = w_in[...].astype(F32).T
    W1T[...] = w1.astype(BF16)
    W1H[...] = (0.5 * w1).astype(BF16)
    w2 = w_mid[...].astype(F32)
    W2H[...] = (0.5 * w2).astype(BF16)
    W2TH[...] = (0.5 * w2.T).astype(BF16)

    def column(row):
        return jnp.broadcast_to(row, (128, row.shape[1])).T

    B1[...] = column(0.5 * b_in[...])
    B2[...] = column(0.5 * b_mid[...])
    for i in range(hid // 128):
        WO[128 * i : 128 * i + 128, :] = column(w_out[i : i + 1, :].astype(F32))
    A1[hid:, :] = jnp.ones((A1.shape[0] - hid, atoms), BF16)
    U[...] = jnp.ones_like(U)
    U[1:4, :] = pos[...]
    U[5:8, :] = pos[...]

    own = l * box_dev + iota((lbox.shape[0], box_dev), 1)
    src = lbox[...]
    dims = (8, 8, n_leaf * box_dev // 64)
    dx, dy, dz = [
        coord(src) + limg[i] * dims[i] - coord(own)
        for i, coord in enumerate([lambda b: b & 7, lambda b: (b >> 3) & 7, lambda b: b >> 6])
    ]
    LCODE[...] = ((dz + 2) * 5 + dy + 2) * 8 + 2 - dx
    sub = iota((8, 128), 0)

    def mask_step(k, masks):
        row = LCODE[pl.ds(k, 1), :] - sub
        return tuple(m + jnp.where(row == 8 * i, 1.0, 0.0) for i, m in enumerate(masks))

    masks = lax.fori_loop(
        0, lbox.shape[0], mask_step, tuple(jnp.zeros((8, 128), F32) for _ in range(n_grp)), unroll=4
    )
    G[...] = jnp.zeros_like(G)
    for i in range(n_grp):
        F[8 * i : 8 * i + 8, :] = masks[i]
    for i in range(n_grp):
        for j in range(5):
            other = 8 * (n_grp - 1 - i) + 4 - j
            G[8 * i + j : 8 * i + j + 1, :] = F[other : other + 1, :]

    def scale_row(cols):
        return (0.5 * COUPLING) * ew[:, cols]

    def one_hot(index, n):
        return jnp.where(iota((n, chunk), 0) == index, 1.0, 0.0).astype(BF16)

    def head(c):
        feat_copy(c).wait()
        at = pl.ds(pl.multiple_of(c * chunk, chunk), chunk)
        h = mm(W1H[...], X[at, :], NT) + tile_lanes(B1[...], chunk)
        t = jnp.tanh(h)
        a = (h + h * t).astype(BF16)
        t = t.astype(BF16)
        A1[:hid, at] = a
        SL1[:, at] = (1 + a) + t * (1 - a)
        h = mm(W2TH[...], a) + tile_lanes(B2[...], chunk)
        t = jnp.tanh(h)
        wo = tile_lanes(WO[...], chunk)
        a = h + h * t
        Q[:, at] = jnp.sum(a * wo, 0, keepdims=True)
        a = a.astype(BF16)
        A2[:, at] = a
        t = t.astype(BF16)
        SL2[:, at] = ((1 + a) + t * (1 - a)) * (0.5 * wo).astype(BF16)

    def before_place(c):
        cols = pl.ds(pl.multiple_of(c * chunk, chunk), chunk)
        s = sslot[:, cols]
        src_leaf = (s >> cap_bits) & (n_leaf - 1)
        row = src_leaf * n_graph + (s >> (cap_bits + leaf_bits))
        OD[:, cols] = one_hot(row, n_leaf * n_graph)
        q = Q[:, cols]
        sub = iota((8, chunk), 0)
        vals = U[:, cols] * jnp.where(sub < 4, q, scale_row(cols) * q)
        hi = vals.astype(BF16).astype(F32)
        lo = vals - hi
        masks = [src_leaf == i for i in range(n_leaf)]
        blocks = [jnp.where(m, hi, 0.0) for m in masks] + [jnp.where(m, lo, 0.0) for m in masks]
        BLK[:, cols] = jnp.concatenate(blocks, 0).astype(BF16)

    def before_grad(c):
        cols = pl.ds(pl.multiple_of(c * chunk, chunk), chunk)
        slope = mm(W2H[...], SL2[:, cols]) * SL1[:, cols].astype(F32)
        SL1[:, cols] = slope.astype(BF16)

    def first_leg():
        pl.semaphore_wait(bar, n_leaf + n_graph - 2)
        to_graph(
            0,
            lambda peer: CODE.at[pl.ds(pl.multiple_of(peer * code_rows, code_rows), code_rows)],
            CA.at[g],
        )
        rows = 8 * half_grp
        send(2, G.at[pl.ds(0, rows)], GN.at[0], (g, leaf_peer(1)))
        send(3, G.at[pl.ds(8 * n_grp - rows, rows)], GN.at[1], (g, leaf_peer(n_leaf - 1)))

    half = 128 // cap

    def second_leg():
        wait_on(rsem.at[0], CA.at[pl.ds(0, n_graph - 1)])
        flat = CA[...]
        for r in range(code_rows):
            CB[r] = flat[:, r, :]
        CS[l] = CB[l // half]
        to_leaf(1, lambda peer: CB.at[peer // half], CS.at[l])

    leg_at = (n_chunks * 4 // 16, n_chunks * 10 // 16)

    @pl.loop(0, n_chunks)
    def _(c):
        pl.when(c == leg_at[0])(first_leg)
        pl.when(c == leg_at[1])(second_leg)
        head(c)

    pl.loop(0, n_chunks)(before_place)

    wait_on(rsem.at[1], CS.at[pl.ds(0, n_leaf - 1)])
    codes = CS[...].reshape(n_leaf * n_graph, 128).T
    mine = codes[:cap]
    for i in range(1, half):
        mine = jnp.where(lax.rem(l, half) == i, codes[i * cap : (i + 1) * cap], mine)
    mine = mine.astype(BF16)
    MACC[...] = jnp.zeros_like(MACC)

    def place(c):
        cols = pl.ds(pl.multiple_of(c * chunk, chunk), chunk)
        picked = mm(mine, OD[:, cols])
        in_row = iota((cap, chunk), 0) == (sslot[:, cols] & (cap - 1))
        atom_box = jnp.sum(jnp.where(in_row, picked, 0.0), 0, keepdims=True)
        ob = one_hot(atom_box.astype(jnp.int32), box_dev)
        OB[:, cols] = ob
        MACC[...] += mm(BLK[:, cols], ob, NT)

    pl.loop(0, n_chunks)(place)

    rows = n_leaf * 8
    part = MACC[:rows, :] + MACC[rows:, :]
    MX[8 : rows + 8, :] = part
    MX[:8, :] = part[rows - 8 :]
    MX[rows + 8 :, :] = part[:8]
    P1[l] = MX[pl.ds(pl.multiple_of(l * 8, 8), 24), :]
    to_leaf(4, lambda peer: MX.at[pl.ds(pl.multiple_of(peer * 8, 8), 24)], P1.at[l])

    wait_on(rsem.at[2], GN.at[0])
    wait_on(rsem.at[3], GN.at[1])
    for i in range(n_grp):
        at = pl.ds(8 * i, 8)
        slabs = [None, shift_x(G[at, :]), None]
        if i < half_grp:
            slabs[0] = shift_x(GN[0, at, :])
        if i >= n_grp - half_grp:
            slabs[2] = shift_x(GN[1, pl.ds(8 * (i - n_grp + half_grp), 8), :])
        R[at, :] = shift_y(shift_z(slabs, i // 5 - 2), i % 5 - 2)
    ACC[...] = jnp.zeros_like(ACC)
    OGACC[...] = jnp.zeros_like(OGACC)
    IBACC[...] = jnp.zeros_like(IBACC)
    cut = [n_chunks * i // 4 for i in range(5)]
    pl.loop(cut[0], cut[2])(before_grad)

    wait_on(rsem.at[4], P1.at[pl.ds(0, n_leaf - 1)])
    total = jnp.sum(P1[...], 0)
    S1[...] = total
    P2[g] = total
    to_graph(5, lambda peer: S1, P2.at[g])
    pl.loop(cut[2], cut[3])(before_grad)
    wait_on(rsem.at[5], P2.at[pl.ds(0, n_graph - 1)])
    total = jnp.sum(P2[...], 0)

    shifted = []
    for ch in range(8):
        slabs = [
            shift_x(jnp.broadcast_to(total[8 * s + ch : 8 * s + ch + 1], (8, 128))) for s in range(3)
        ]
        shifted.append([shift_z(slabs, d) for d in range(-2, 3)])
    off_x = (2 - iota((8, 128), 0)).astype(F32)
    sums = [jnp.zeros((8, 128), F32) for _ in range(8)]
    for i in range(n_grp):
        off_z, off_y = i // 5 - 2, i % 5 - 2
        dist = jnp.maximum(off_x * off_x + float(off_z * off_z + off_y * off_y), 1.0)
        inv = lax.rsqrt(dist)
        cube = inv * inv * inv
        three = 3.0 * inv * inv
        for base, mask in ((0, F), (4, R)):
            m = mask[8 * i : 8 * i + 8, :]
            q0, q1, q2, q3 = [
                m * shift_y(shifted[base + j][off_z + 2], off_y) for j in range(4)
            ]
            proj = off_x * q1 + float(off_y) * q2 + float(off_z) * q3
            sums[base] += q0 * inv - proj * cube
            radial = q0 - three * proj
            sums[base + 1] += (radial * off_x + q1) * cube
            sums[base + 2] += (radial * float(off_y) + q2) * cube
            sums[base + 3] += (radial * float(off_z) + q3) * cube
    for j in range(8):
        TO[j : j + 1, :] = jnp.sum(sums[j], 0, keepdims=True)
    TB[l] = TO[...]
    to_leaf(6, lambda peer: TO, TB.at[l])
    pl.loop(cut[3], cut[4])(before_grad)
    wait_on(rsem.at[6], TB.at[pl.ds(0, n_leaf - 1)])
    table = TB[...].reshape(rows, 128)
    hi = table.astype(BF16)
    table = jnp.concatenate([hi, (table - hi.astype(F32)).astype(BF16)], 0)

    def backward(c):
        cols = pl.ds(pl.multiple_of(c * chunk, chunk), chunk)
        src_leaf = (sslot[:, cols] >> cap_bits) & (n_leaf - 1)
        got = mm(table, OB[:, cols])
        got = got[:rows] + got[rows:]
        field = jnp.zeros((8, chunk), F32)
        for i in range(n_leaf):
            field += jnp.where(src_leaf == i, got[8 * i : 8 * i + 8], 0.0)
        sub = iota((8, chunk), 0)
        terms = field * U[:, cols]
        q = Q[:, cols]
        w = scale_row(cols)
        grad = jnp.sum(terms * jnp.where(sub < 4, w, 1.0), 0, keepdims=True)
        force = field * jnp.where(sub < 4, w * q, q)
        force = force + pltpu.roll(force, 4, 0)
        pgrad[:, cols] = force[1:4]
        grad = jnp.broadcast_to(grad, (16, chunk)).astype(BF16)[None]

        def scaled(ref):
            x = ref[:, cols].reshape(hid // 16, 16, chunk) * grad
            return x.reshape(hid, chunk)

        ACC[0] += mm(A1[:, cols], scaled(SL2), NT)
        slope = scaled(SL1)
        SL1[:, cols] = slope
        ACC[1, :hid, :] += mm(slope, X[cols, :])
        IBACC[...] += fold_lanes(slope.astype(F32))
        OGACC[...] += fold_lanes(scaled(A2).astype(F32))

    pl.loop(0, n_chunks)(backward)

    BOTH[...] = ACC[:, :hid, :].astype(BF16)
    to_core(7, BOTH.at[1 - core], RX)

    def to_row(columns):
        return jnp.sum(columns.T, 0, keepdims=True)

    BV[...] = jnp.zeros_like(BV)
    vectors = (ACC[0, hid : hid + 1, :], to_row(OGACC[...]), to_row(IBACC[...]))
    for i, vector in enumerate(vectors):
        for j in range(hid // 128):
            at = 2 * i + j
            BV[at : at + 1, :] = vector[:, 128 * j : 128 * j + 128]
    BX[core] = BV[...]
    to_core(8, BV, BX.at[core])
    wait_on(rsem.at[7], RX)
    SB[...] = (ACC[core, :hid, :] + RX[...].astype(F32)).astype(BF16)
    RM[l] = SB[pl.ds(pl.multiple_of(l * wrow, wrow), wrow), :]
    to_leaf(9, lambda peer: SB.at[pl.ds(pl.multiple_of(peer * wrow, wrow), wrow)], RM.at[l])
    wait_on(rsem.at[8], BV)
    BC[...] = BX[0] + BX[1]
    BL[l] = BC[...]
    to_leaf(10, lambda peer: BC, BL.at[l])

    def out_copy(c):
        rows = pl.ds(c * chunk, chunk)
        return pltpu.make_async_copy(X.at[rows], fgrad.at[rows], osem.at[c])

    def backward_row(c):
        at = pl.ds(pl.multiple_of(c * chunk, chunk), chunk)
        X[at, :] = mm(SL1[:, at], W1T[...], TN).astype(BF16)
        out_copy(c).start()

    def sum_leaf():
        wait_on(rsem.at[9], RM.at[pl.ds(0, n_leaf - 1)])
        wait_on(rsem.at[10], BL.at[pl.ds(0, n_leaf - 1)])
        GS[...] = jnp.sum(RM[...].astype(F32), 0).astype(BF16)
        GM[zpos] = GS[...]
        to_z(11, GS, GM.at[zpos])
        BS[...] = jnp.sum(BL[...], 0)
        BG[zpos] = BS[...]
        to_z(12, BS, BG.at[zpos])

    @pl.loop(0, n_chunks)
    def _(c):
        backward_row(c)

    sum_leaf()
    wait_on(rsem.at[11], GM.at[pl.ds(0, n_z - 1)])
    AS[...] = jnp.sum(GM[...].astype(F32), 0).astype(BF16)
    AM[l] = AS[...]
    to_leaf(13, lambda peer: AS, AM.at[l])
    wait_on(rsem.at[12], BG.at[pl.ds(0, n_z - 1)])
    bias = jnp.sum(BG[...], 0)
    for i, out in enumerate((midb, outg, inb)):
        for j in range(hid // 128):
            out[:, 128 * j : 128 * j + 128] = bias[2 * i + j : 2 * i + j + 1]
    wait_on(rsem.at[13], AM.at[pl.ds(0, n_leaf - 1)])
    to_core(14, AM, AO)
    mine = AM[...].astype(F32).reshape(hid, hid)
    wait_on(rsem.at[14], AO)
    other = AO[...].astype(F32).reshape(hid, hid)
    midg[...] = jnp.where(core == 0, mine, other)
    ing[...] = jnp.where(core == 0, other, mine).T

    leaf_sent = pl.ds(0, n_leaf - 1)
    graph_sent = pl.ds(0, n_graph - 1)
    z_sent = pl.ds(0, n_z - 1)
    for k, view in enumerate(
        (
            CA.at[graph_sent], CS.at[leaf_sent], GN.at[0], GN.at[1], P1.at[leaf_sent],
            P2.at[graph_sent], TB.at[leaf_sent], RX, BV, RM.at[leaf_sent], BL.at[leaf_sent],
            GM.at[z_sent], BG.at[z_sent], AM.at[leaf_sent], AO,
        )
    ):
        wait_on(ssem.at[k], view)

    @pl.loop(0, n_chunks)
    def _(c):
        out_copy(c).wait()


def copy_out(pieces, *refs):
    n = (len(refs) - 2) // 3
    legs = []
    sems = refs[-2:]
    for src, dst, held in zip(refs[:n], refs[n : 2 * n], refs[2 * n : 3 * n]):
        parts = pieces if src.shape[0] > 1024 else 1
        rows = src.shape[0] // parts
        for i in range(parts):
            at = pl.ds(i * rows, rows)
            k = len(legs)
            legs.append(
                (
                    pltpu.make_async_copy(src.at[at], held.at[at], sems[0].at[k]),
                    pltpu.make_async_copy(held.at[at], dst.at[at], sems[1].at[k]),
                )
            )
    for load, _ in legs:
        load.start()
    for load, store in legs:
        load.wait()
        store.start()
    for _, store in legs:
        store.wait()


def body(
    features, positions, energy_weight, send_slot, tile_slot, box_count, list_box, list_image,
    w_in, b_in, w_mid, b_mid, w_out,
):
    n_graph, n_leaf = lax.axis_size("graph"), lax.axis_size("leaf")
    atoms, feat = features.shape
    hid = w_in.shape[1]
    chunk = min(CHUNK, atoms // 4)
    n_grp = 25
    n_z = n_graph // 2
    code_rows = n_leaf * (atoms // (n_graph * n_leaf)) // 128
    wrow = hid // n_leaf
    vmem = pl.BlockSpec(memory_space=pltpu.VMEM)
    any_space = pl.BlockSpec(memory_space=pl.ANY)
    smem = pl.BlockSpec(memory_space=pltpu.SMEM)

    def v(shape, dtype=F32):
        return pltpu.VMEM(shape, dtype)

    scratch = [
        v((atoms, feat), BF16), v((hid + 16, atoms), BF16), v((hid, atoms), BF16),
        v((hid, atoms), BF16), v((hid, atoms), BF16), v((128, atoms), BF16),
        v((n_leaf * n_graph, atoms), BF16), v((n_leaf * 16, atoms), BF16),
        v((8, atoms)), v((1, atoms)),
        v((hid, feat), BF16), v((hid, feat), BF16), v((hid, hid), BF16), v((hid, hid), BF16),
        v((hid, 128)), v((hid, 128)), v((hid, 128)),
        v((atoms // 128, 128)), v((n_graph, code_rows, 128)), v((code_rows, n_graph, 128)),
        v((n_leaf, n_graph, 128)),
        v((8 * n_grp, 128)), v((8 * n_grp, 128)), v((2, 80, 128)), v((8 * n_grp, 128)),
        v((list_box.shape[1], 128), jnp.int32),
        v((n_leaf * 16, 128)),
        v((n_leaf * 8 + 16, 128)), v((n_leaf, 24, 128)), v((24, 128)), v((n_graph, 24, 128)),
        v((8, 128)), v((n_leaf, 8, 128)),
        v((2, hid + 16, hid)), v((hid, 128)), v((hid, 128)),
        v((2, hid, hid), BF16), v((hid, hid), BF16), v((hid, hid), BF16),
        v((n_leaf, wrow, hid), BF16), v((wrow, hid), BF16), v((n_z, wrow, hid), BF16),
        v((wrow, hid), BF16), v((n_leaf, wrow, hid), BF16), v((n_leaf, wrow, hid), BF16),
        v((8, 128)), v((2, 8, 128)), v((8, 128)), v((n_leaf, 8, 128)), v((8, 128)),
        v((n_z, 8, 128)),
        pltpu.SemaphoreType.DMA((atoms // chunk,)), pltpu.SemaphoreType.DMA((atoms // chunk,)),
        pltpu.SemaphoreType.DMA((15,)), pltpu.SemaphoreType.DMA((15,)),
    ]
    sds = jax.ShapeDtypeStruct
    shapes = (
        sds((atoms, feat), BF16), sds((3, atoms), F32),
        sds((feat, hid), F32), sds((1, hid), F32),
        sds((hid, hid), F32), sds((1, hid), F32), sds((1, hid), F32),
    )
    outs = pl.pallas_call(
        functools.partial(kernel, n_graph, n_leaf, chunk, n_grp),
        out_shape=shapes,
        in_specs=[any_space, vmem, vmem, vmem, vmem, smem] + [vmem] * 7,
        out_specs=(any_space,) + (vmem,) * 6,
        scratch_shapes=scratch,
        compiler_params=pltpu.CompilerParams(
            collective_id=0, has_side_effects=True, vmem_limit_bytes=56 * 1024 * 1024
        ),
        name="latent_charge",
    )(
        features, positions, energy_weight.reshape(1, atoms), send_slot.reshape(1, atoms),
        tile_slot.reshape(atoms // 128, 128), box_count.reshape(1, -1), list_box.T,
        list_image.transpose(0, 2, 1), w_in, b_in.reshape(1, hid), w_mid, b_mid.reshape(1, hid),
        w_out.reshape(hid // 128, 128),
    )
    pieces = 8
    legs = pieces + len(shapes)
    outs = pl.pallas_call(
        functools.partial(copy_out, pieces),
        out_shape=shapes,
        in_specs=[any_space] * len(shapes),
        out_specs=(any_space,) * len(shapes),
        scratch_shapes=[v(x.shape, x.dtype) for x in shapes]
        + [pltpu.SemaphoreType.DMA((legs,)), pltpu.SemaphoreType.DMA((legs,))],
        compiler_params=pltpu.CompilerParams(vmem_limit_bytes=56 * 1024 * 1024),
        name="results",
    )(*outs)
    fgrad, pgrad, ing, inb, midg, midb, outg = outs
    return (fgrad, pgrad, ing, inb.reshape(hid), midg, midb.reshape(hid), outg.reshape(hid))


def solution(mesh):
    placed = (
        P(("graph", "leaf"), None),
        P(None, ("graph", "leaf")),
        P(("graph", "leaf")),
        P(("graph", "leaf")),
        P(("graph", "leaf")),
        P("leaf", "graph"),
        P("leaf", None),
        P(None, "leaf", None),
        P(), P(), P(), P(), P(),
    )
    return jax.shard_map(
        body,
        mesh=mesh,
        in_specs=placed,
        out_specs=(P(("graph", "leaf"), None), P(None, ("graph", "leaf")), P(), P(), P(), P(), P()),
        check_vma=False,
    )
```

time: 92.8 us -> 75.3 us (0.81)
  local copies, waits for them, and re-layouts: 14.1 us -> 0 us
  Pallas kernels: 77.7 us -> 74.5 us
    unnamed x22 -> x0, local copies, waits for them, and re-layouts: 12.9 us -> none
    pallas_call x1, Pallas kernels: 77.7 us -> 70.2 us  [body(): pl.pallas_call(functools.partial(kernel, n_graph, n_leaf, chunk, n_grp),...]
    pallas_call x0 -> x1, Pallas kernels: none -> 4.3 us  [body(): pl.pallas_call(functools.partial(copy_out, pieces), out_shape=shapes, in_...]
    reshape x1 -> x0, local copies, waits for them, and re-layouts: 1.22 us -> none  [body(): w_out.reshape(1, hid)]
where the time goes in v2:
time: 75.3 us; the launch traced here: 75.1 us
  Pallas kernels  74.5 us (99%)
    pallas_call x1, Pallas kernels, body(): pl.pallas_call(functools.partial(kernel, n_graph, n_leaf, chunk, n_grp),...  70.2 us
    pallas_call x1, Pallas kernels, body(): pl.pallas_call(functools.partial(copy_out, pieces), out_shape=shapes, in_...  4.3 us

profile of v2, /device:TPU:1, one launch (start us, length us, event | category | flops | bytes accessed | tf_op | source)
XLA Modules:
  0.0 75.1 jit_solution(12083352167664591309)
XLA Ops:
  0.6 70.2 %latent_charge.1 = (bf16[8192,256]{1,0:T(8,128)(2,1)}, f32[3,8192]{1,0:T(4,128)}, f32[256,256]{1,0:T(8,128)}, f32[1,256]{1,0:T(1,128)}, f32[256,256]{1,0:T(8,128)}, /*index=5*/f32[1,256]{1,0:T(1,128)}, f32[1,256]{1,0:T(1,128)}) custom-call(bf16[8192,256]{1,0:T(8,128)(2,1)} %feat.1, f32[3,8192]{1,0:T(4,128)} %pos.1, f32[1,8192]{1,0:T(1,128)} %bitcast.13, ...), custom_call_target="tpu_custom_call" | custom-call | tf_op jit(solution)/shard_map/latent_charge/pallas_call | solution.py:547
  70.8 4.3 %results.1 = (bf16[8192,256]{1,0:T(8,128)(2,1)}, f32[3,8192]{1,0:T(4,128)}, f32[256,256]{1,0:T(8,128)}, f32[1,256]{1,0:T(1,128)}, f32[256,256]{1,0:T(8,128)}, /*index=5*/f32[1,256]{1,0:T(1,128)}, f32[1,256]{1,0:T(1,128)}) custom-call(bf16[8192,256]{1,0:T(8,128)(2,1)} %get-tuple-element.21.refs_0_, f32[3,8192]{1,0:T(4,128)} %get-tuple-element.22.refs_1_, ...), custom_call_target="tpu_custom_call" | custom-call | tf_op jit(solution)/shard_map/results/pallas_call | solution.py:565

commit v3 on v2

--- a/solution.py
+++ b/solution.py
@@ -12,7 +12,8 @@
 BF16 = jnp.bfloat16
 COUPLING = 0.5
 SLOT_DEV = 128
-CHUNK = 512
+HEAD_CHUNK = 1024
+CHUNK = 2048
 NT = (((1,), (1,)), ((), ()))
 NN = (((1,), (0,)), ((), ()))
 TN = (((0,), (0,)), ((), ()))
@@ -65,15 +66,22 @@
 
 
 def kernel(
-    n_graph, n_leaf, chunk, n_grp,
-    feat, pos, ew, sslot, tslot, count, lbox, limg, w_in, b_in, w_mid, b_mid, w_out,
-    fgrad, pgrad, ing, inb, midg, midb, outg,
+    n_graph, n_leaf, head_chunk, chunk, n_grp,
+    feat, *refs,
+):
+    ins, refs = refs[:12], refs[12:]
+    outs, refs = refs[:4], refs[4:]
+    (pos, ew, sslot, tslot, count, lbox, limg, w_in, b_in, w_mid, b_mid, w_out), refs = (
+        refs[:12], refs[12:],
+    )
+    fgrad, pgrad, mats, bias_out = outs
+    (
     X, A1, SL1, A2, SL2, OB, OD, BLK, U, Q, W1H, W1T, W2TH, W2H, B1, B2, WO,
     CODE, CA, CB, CS, F, G, GN, R, LCODE, MACC, MX, P1, S1, P2, TO, TB,
     ACC, OGACC, IBACC, BOTH, RX, SB, RM, GS, GM, AS, AM, AO,
-    BV, BX, BC, BL, BS, BG,
-    xsem, osem, ssem, rsem,
-):
+    BV, BX, BC, BL, BS, BG, BF, GR, FIELD, PG,
+    xsem, osem, isem, ssem, rsem,
+    ) = refs
     g = lax.axis_index("graph")
     l = lax.axis_index("leaf")
     core = lax.rem(g, 2)
@@ -87,6 +95,7 @@
     box_dev = 128
     wrow = hid // n_leaf
     n_z = n_graph // 2
+    n_heads = atoms // head_chunk
     n_chunks = atoms // chunk
     half_grp = 2 * (n_grp // 5)
 
@@ -135,12 +144,24 @@
         )
 
     def feat_copy(c):
-        rows = pl.ds(c * chunk, chunk)
+        rows = pl.ds(c * head_chunk, head_chunk)
         return pltpu.make_async_copy(feat.at[rows], X.at[rows], xsem.at[c])
 
-    @pl.loop(0, n_chunks)
+    fetches = [
+        pltpu.make_async_copy(src, dst, isem.at[i])
+        for i, (src, dst) in enumerate(
+            zip(ins, (pos, ew, sslot, tslot, count, lbox, limg, w_in, b_in, w_mid, b_mid, w_out))
+        )
+    ]
+    for fetch in fetches:
+        fetch.start()
+
+    @pl.loop(0, n_heads)
     def _(c):
         feat_copy(c).start()
+
+    for fetch in fetches:
+        fetch.wait()
 
     slot = tslot[...]
     box = slot >> 7
@@ -204,16 +225,16 @@
 
     def head(c):
         feat_copy(c).wait()
-        at = pl.ds(pl.multiple_of(c * chunk, chunk), chunk)
-        h = mm(W1H[...], X[at, :], NT) + tile_lanes(B1[...], chunk)
+        at = pl.ds(pl.multiple_of(c * head_chunk, head_chunk), head_chunk)
+        h = mm(W1H[...], X[at, :], NT) + tile_lanes(B1[...], head_chunk)
         t = jnp.tanh(h)
         a = (h + h * t).astype(BF16)
         t = t.astype(BF16)
         A1[:hid, at] = a
         SL1[:, at] = (1 + a) + t * (1 - a)
-        h = mm(W2TH[...], a) + tile_lanes(B2[...], chunk)
+        h = mm(W2TH[...], a) + tile_lanes(B2[...], head_chunk)
         t = jnp.tanh(h)
-        wo = tile_lanes(WO[...], chunk)
+        wo = tile_lanes(WO[...], head_chunk)
         a = h + h * t
         Q[:, at] = jnp.sum(a * wo, 0, keepdims=True)
         a = a.astype(BF16)
@@ -262,9 +283,9 @@
         CS[l] = CB[l // half]
         to_leaf(1, lambda peer: CB.at[peer // half], CS.at[l])
 
-    leg_at = (n_chunks * 4 // 16, n_chunks * 10 // 16)
-
-    @pl.loop(0, n_chunks)
+    leg_at = (n_heads * 2 // 16, n_heads * 10 // 16)
+
+    @pl.loop(0, n_heads)
     def _(c):
         pl.when(c == leg_at[0])(first_leg)
         pl.when(c == leg_at[1])(second_leg)
@@ -367,15 +388,13 @@
         field = jnp.zeros((8, chunk), F32)
         for i in range(n_leaf):
             field += jnp.where(src_leaf == i, got[8 * i : 8 * i + 8], 0.0)
+        FIELD[:, cols] = field
         sub = iota((8, chunk), 0)
-        terms = field * U[:, cols]
-        q = Q[:, cols]
-        w = scale_row(cols)
-        grad = jnp.sum(terms * jnp.where(sub < 4, w, 1.0), 0, keepdims=True)
-        force = field * jnp.where(sub < 4, w * q, q)
-        force = force + pltpu.roll(force, 4, 0)
-        pgrad[:, cols] = force[1:4]
-        grad = jnp.broadcast_to(grad, (16, chunk)).astype(BF16)[None]
+        terms = field * U[:, cols] * jnp.where(sub < 4, scale_row(cols), 1.0)
+        grad = jnp.sum(terms, 0, keepdims=True)
+        grad = jnp.broadcast_to(grad, (16, chunk)).astype(BF16)
+        GR[:, cols] = grad
+        grad = grad[None]
 
         def scaled(ref):
             x = ref[:, cols].reshape(hid // 16, 16, chunk) * grad
@@ -385,8 +404,6 @@
         slope = scaled(SL1)
         SL1[:, cols] = slope
         ACC[1, :hid, :] += mm(slope, X[cols, :])
-        IBACC[...] += fold_lanes(slope.astype(F32))
-        OGACC[...] += fold_lanes(scaled(A2).astype(F32))
 
     pl.loop(0, n_chunks)(backward)
 
@@ -396,6 +413,29 @@
     def to_row(columns):
         return jnp.sum(columns.T, 0, keepdims=True)
 
+    wait_on(rsem.at[7], RX)
+    SB[...] = (ACC[core, :hid, :] + RX[...].astype(F32)).astype(BF16)
+    RM[l] = SB[pl.ds(pl.multiple_of(l * wrow, wrow), wrow), :]
+    to_leaf(9, lambda peer: SB.at[pl.ds(pl.multiple_of(peer * wrow, wrow), wrow)], RM.at[l])
+    def out_copy(c):
+        rows = pl.ds(c * chunk, chunk)
+        return pltpu.make_async_copy(X.at[rows], fgrad.at[rows], osem.at[c])
+
+    def backward_row(c):
+        at = pl.ds(pl.multiple_of(c * chunk, chunk), chunk)
+        X[at, :] = mm(SL1[:, at], W1T[...], TN).astype(BF16)
+        out_copy(c).start()
+        IBACC[...] += fold_lanes(SL1[:, at].astype(F32))
+        og = A2[:, at].reshape(hid // 16, 16, chunk) * GR[:, at][None]
+        OGACC[...] += fold_lanes(og.reshape(hid, chunk).astype(F32))
+        q = Q[:, at]
+        force = FIELD[:, at] * jnp.where(iota((8, chunk), 0) < 4, scale_row(at) * q, q)
+        force = force + pltpu.roll(force, 4, 0)
+        PG[:, at] = force[1:4]
+
+    pl.loop(0, n_chunks)(backward_row)
+    force_copy = pltpu.make_async_copy(PG, pgrad, isem.at[0])
+    force_copy.start()
     BV[...] = jnp.zeros_like(BV)
     vectors = (ACC[0, hid : hid + 1, :], to_row(OGACC[...]), to_row(IBACC[...]))
     for i, vector in enumerate(vectors):
@@ -404,95 +444,88 @@
             BV[at : at + 1, :] = vector[:, 128 * j : 128 * j + 128]
     BX[core] = BV[...]
     to_core(8, BV, BX.at[core])
-    wait_on(rsem.at[7], RX)
-    SB[...] = (ACC[core, :hid, :] + RX[...].astype(F32)).astype(BF16)
-    RM[l] = SB[pl.ds(pl.multiple_of(l * wrow, wrow), wrow), :]
-    to_leaf(9, lambda peer: SB.at[pl.ds(pl.multiple_of(peer * wrow, wrow), wrow)], RM.at[l])
     wait_on(rsem.at[8], BV)
     BC[...] = BX[0] + BX[1]
     BL[l] = BC[...]
     to_leaf(10, lambda peer: BC, BL.at[l])
 
-    def out_copy(c):
-        rows = pl.ds(c * chunk, chunk)
-        return pltpu.make_async_copy(X.at[rows], fgrad.at[rows], osem.at[c])
-
-    def backward_row(c):
-        at = pl.ds(pl.multiple_of(c * chunk, chunk), chunk)
-        X[at, :] = mm(SL1[:, at], W1T[...], TN).astype(BF16)
-        out_copy(c).start()
-
-    def sum_leaf():
-        wait_on(rsem.at[9], RM.at[pl.ds(0, n_leaf - 1)])
-        wait_on(rsem.at[10], BL.at[pl.ds(0, n_leaf - 1)])
-        GS[...] = jnp.sum(RM[...].astype(F32), 0).astype(BF16)
-        GM[zpos] = GS[...]
-        to_z(11, GS, GM.at[zpos])
-        BS[...] = jnp.sum(BL[...], 0)
-        BG[zpos] = BS[...]
-        to_z(12, BS, BG.at[zpos])
-
-    @pl.loop(0, n_chunks)
-    def _(c):
-        backward_row(c)
-
-    sum_leaf()
+    wait_on(rsem.at[9], RM.at[pl.ds(0, n_leaf - 1)])
+    GS[...] = jnp.sum(RM[...].astype(F32), 0).astype(BF16)
+    GM[zpos] = GS[...]
+    to_z(11, GS, GM.at[zpos])
     wait_on(rsem.at[11], GM.at[pl.ds(0, n_z - 1)])
     AS[...] = jnp.sum(GM[...].astype(F32), 0).astype(BF16)
     AM[l] = AS[...]
     to_leaf(13, lambda peer: AS, AM.at[l])
+    wait_on(rsem.at[10], BL.at[pl.ds(0, n_leaf - 1)])
+    BS[...] = jnp.sum(BL[...], 0)
+    BG[zpos] = BS[...]
+    to_z(12, BS, BG.at[zpos])
     wait_on(rsem.at[12], BG.at[pl.ds(0, n_z - 1)])
-    bias = jnp.sum(BG[...], 0)
-    for i, out in enumerate((midb, outg, inb)):
-        for j in range(hid // 128):
-            out[:, 128 * j : 128 * j + 128] = bias[2 * i + j : 2 * i + j + 1]
+    BF[...] = jnp.sum(BG[...], 0)
+    bias_copy = pltpu.make_async_copy(BF, bias_out, isem.at[1])
+    bias_copy.start()
     wait_on(rsem.at[13], AM.at[pl.ds(0, n_leaf - 1)])
     to_core(14, AM, AO)
-    mine = AM[...].astype(F32).reshape(hid, hid)
-    wait_on(rsem.at[14], AO)
-    other = AO[...].astype(F32).reshape(hid, hid)
-    midg[...] = jnp.where(core == 0, mine, other)
-    ing[...] = jnp.where(core == 0, other, mine).T
+    mine_copy = pltpu.make_async_copy(AM, mats.at[core], isem.at[2])
+    mine_copy.start()
 
     leaf_sent = pl.ds(0, n_leaf - 1)
     graph_sent = pl.ds(0, n_graph - 1)
     z_sent = pl.ds(0, n_z - 1)
-    for k, view in enumerate(
-        (
-            CA.at[graph_sent], CS.at[leaf_sent], GN.at[0], GN.at[1], P1.at[leaf_sent],
-            P2.at[graph_sent], TB.at[leaf_sent], RX, BV, RM.at[leaf_sent], BL.at[leaf_sent],
-            GM.at[z_sent], BG.at[z_sent], AM.at[leaf_sent], AO,
-        )
-    ):
+    sent = {
+        0: CA.at[graph_sent], 1: CS.at[leaf_sent], 2: GN.at[0], 3: GN.at[1], 4: P1.at[leaf_sent],
+        5: P2.at[graph_sent], 6: TB.at[leaf_sent], 7: RX, 8: BV, 9: RM.at[leaf_sent],
+        10: BL.at[leaf_sent], 11: GM.at[z_sent], 12: BG.at[z_sent], 13: AM.at[leaf_sent], 14: AO,
+    }
+    for k, view in sent.items():
         wait_on(ssem.at[k], view)
 
     @pl.loop(0, n_chunks)
     def _(c):
         out_copy(c).wait()
 
-
-def copy_out(pieces, *refs):
-    n = (len(refs) - 2) // 3
-    legs = []
-    sems = refs[-2:]
-    for src, dst, held in zip(refs[:n], refs[n : 2 * n], refs[2 * n : 3 * n]):
-        parts = pieces if src.shape[0] > 1024 else 1
-        rows = src.shape[0] // parts
-        for i in range(parts):
-            at = pl.ds(i * rows, rows)
-            k = len(legs)
-            legs.append(
-                (
-                    pltpu.make_async_copy(src.at[at], held.at[at], sems[0].at[k]),
-                    pltpu.make_async_copy(held.at[at], dst.at[at], sems[1].at[k]),
-                )
-            )
-    for load, _ in legs:
+    force_copy.wait()
+    bias_copy.wait()
+    wait_on(rsem.at[14], AO)
+    other_copy = pltpu.make_async_copy(AO, mats.at[1 - core], isem.at[3])
+    other_copy.start()
+    mine_copy.wait()
+    other_copy.wait()
+
+
+def finish(
+    pieces, fgrad, pgrad, mats, bias, fout, pout, ing, inb, midg, midb, outg,
+    FH, PH, MH, BH, IN, MID, IB, MB, OG, lsem, ssem,
+):
+    rows = FH.shape[0] // pieces
+    legs = [
+        (fgrad.at[pl.ds(i * rows, rows)], FH.at[pl.ds(i * rows, rows)], fout.at[pl.ds(i * rows, rows)])
+        for i in range(pieces)
+    ]
+    legs.append((pgrad, PH, pout))
+    loads = [pltpu.make_async_copy(a, b, lsem.at[i]) for i, (a, b, _) in enumerate(legs)]
+    stores = [pltpu.make_async_copy(b, c, ssem.at[i]) for i, (_, b, c) in enumerate(legs)]
+    last = len(legs)
+    loads.append(pltpu.make_async_copy(mats, MH, lsem.at[last]))
+    loads.append(pltpu.make_async_copy(bias, BH, lsem.at[last + 1]))
+    for load in loads:
         load.start()
-    for load, store in legs:
+    for load, store in zip(loads, stores):
         load.wait()
         store.start()
-    for _, store in legs:
+    for load in loads[last:]:
+        load.wait()
+    hid = MID.shape[0]
+    MID[...] = MH[0].astype(F32).reshape(hid, hid)
+    IN[...] = MH[1].astype(F32).reshape(hid, hid).T
+    for i, row in enumerate((MB, OG, IB)):
+        for j in range(hid // 128):
+            row[:, 128 * j : 128 * j + 128] = BH[2 * i + j : 2 * i + j + 1, :]
+    for i, (a, b) in enumerate(((IN, ing), (MID, midg), (IB, inb), (MB, midb), (OG, outg))):
+        stores.append(pltpu.make_async_copy(a, b, ssem.at[last + i]))
+        stores[-1].start()
+    for store in stores:
         store.wait()
 
 
@@ -503,14 +536,13 @@
     n_graph, n_leaf = lax.axis_size("graph"), lax.axis_size("leaf")
     atoms, feat = features.shape
     hid = w_in.shape[1]
+    head_chunk = min(HEAD_CHUNK, atoms // 4)
     chunk = min(CHUNK, atoms // 4)
     n_grp = 25
     n_z = n_graph // 2
     code_rows = n_leaf * (atoms // (n_graph * n_leaf)) // 128
     wrow = hid // n_leaf
-    vmem = pl.BlockSpec(memory_space=pltpu.VMEM)
     any_space = pl.BlockSpec(memory_space=pl.ANY)
-    smem = pl.BlockSpec(memory_space=pltpu.SMEM)
 
     def v(shape, dtype=F32):
         return pltpu.VMEM(shape, dtype)
@@ -534,9 +566,10 @@
         v((n_leaf, wrow, hid), BF16), v((wrow, hid), BF16), v((n_z, wrow, hid), BF16),
         v((wrow, hid), BF16), v((n_leaf, wrow, hid), BF16), v((n_leaf, wrow, hid), BF16),
         v((8, 128)), v((2, 8, 128)), v((8, 128)), v((n_leaf, 8, 128)), v((8, 128)),
-        v((n_z, 8, 128)),
-        pltpu.SemaphoreType.DMA((atoms // chunk,)), pltpu.SemaphoreType.DMA((atoms // chunk,)),
-        pltpu.SemaphoreType.DMA((15,)), pltpu.SemaphoreType.DMA((15,)),
+        v((n_z, 8, 128)), v((8, 128)), v((16, atoms), BF16), v((8, atoms)), v((3, atoms)),
+        pltpu.SemaphoreType.DMA((atoms // head_chunk,)), pltpu.SemaphoreType.DMA((atoms // chunk,)),
+        pltpu.SemaphoreType.DMA((12,)), pltpu.SemaphoreType.DMA((15,)),
+        pltpu.SemaphoreType.DMA((15,)),
     ]
     sds = jax.ShapeDtypeStruct
     shapes = (
@@ -544,34 +577,41 @@
         sds((feat, hid), F32), sds((1, hid), F32),
         sds((hid, hid), F32), sds((1, hid), F32), sds((1, hid), F32),
     )
-    outs = pl.pallas_call(
-        functools.partial(kernel, n_graph, n_leaf, chunk, n_grp),
-        out_shape=shapes,
-        in_specs=[any_space, vmem, vmem, vmem, vmem, smem] + [vmem] * 7,
-        out_specs=(any_space,) + (vmem,) * 6,
-        scratch_shapes=scratch,
+    mids = (
+        shapes[0], shapes[1], sds((2, n_leaf, wrow, hid), BF16), sds((8, 128), F32),
+    )
+    ins = (
+        positions, energy_weight.reshape(1, atoms), send_slot.reshape(1, atoms),
+        tile_slot.reshape(atoms // 128, 128), box_count.reshape(1, -1), list_box.T,
+        list_image.transpose(0, 2, 1), w_in, b_in.reshape(1, hid), w_mid, b_mid.reshape(1, hid),
+        w_out.reshape(hid // 128, 128),
+    )
+    held = [
+        (pltpu.SMEM if i == 4 else pltpu.VMEM)(x.shape, x.dtype) for i, x in enumerate(ins)
+    ]
+    mids = pl.pallas_call(
+        functools.partial(kernel, n_graph, n_leaf, head_chunk, chunk, n_grp),
+        out_shape=mids,
+        in_specs=[any_space] * 13,
+        out_specs=(any_space,) * 4,
+        scratch_shapes=held + scratch,
         compiler_params=pltpu.CompilerParams(
             collective_id=0, has_side_effects=True, vmem_limit_bytes=56 * 1024 * 1024
         ),
         name="latent_charge",
-    )(
-        features, positions, energy_weight.reshape(1, atoms), send_slot.reshape(1, atoms),
-        tile_slot.reshape(atoms // 128, 128), box_count.reshape(1, -1), list_box.T,
-        list_image.transpose(0, 2, 1), w_in, b_in.reshape(1, hid), w_mid, b_mid.reshape(1, hid),
-        w_out.reshape(hid // 128, 128),
-    )
-    pieces = 8
-    legs = pieces + len(shapes)
+    )(features, *ins)
+    pieces = 4
     outs = pl.pallas_call(
-        functools.partial(copy_out, pieces),
+        functools.partial(finish, pieces),
         out_shape=shapes,
-        in_specs=[any_space] * len(shapes),
+        in_specs=[any_space] * 4,
         out_specs=(any_space,) * len(shapes),
-        scratch_shapes=[v(x.shape, x.dtype) for x in shapes]
-        + [pltpu.SemaphoreType.DMA((legs,)), pltpu.SemaphoreType.DMA((legs,))],
+        scratch_shapes=[v(x.shape, x.dtype) for x in mids]
+        + [v(shapes[i].shape) for i in (2, 4, 3, 5, 6)]
+        + [pltpu.SemaphoreType.DMA((pieces + 3,)), pltpu.SemaphoreType.DMA((pieces + 6,))],
         compiler_params=pltpu.CompilerParams(vmem_limit_bytes=56 * 1024 * 1024),
         name="results",
-    )(*outs)
+    )(*mids)
     fgrad, pgrad, ing, inb, midg, midb, outg = outs
     return (fgrad, pgrad, ing, inb.reshape(hid), midg, midb.reshape(hid), outg.reshape(hid))
 

time: 75.3 us -> 61.4 us (0.82)
  Pallas kernels: 74.5 us -> 60.7 us
    pallas_call x2, Pallas kernels: 74.5 us -> 60.7 us  [the longest x1 57 us: body(): pl.pallas_call(functools.partial(kernel, n_graph, n_leaf, head_chunk, chu...]
where the time goes in v3:
time: 61.4 us; the launch traced here: 61.3 us
  Pallas kernels  60.7 us (99%)
  between operations  0.65 us (1%)
    pallas_call x1, Pallas kernels, body(): pl.pallas_call(functools.partial(kernel, n_graph, n_leaf, head_chunk, chu...  57 us
    pallas_call x1, Pallas kernels, body(): pl.pallas_call(functools.partial(finish, pieces), out_shape=shapes, in_sp...  3.65 us

profile of v3, /device:TPU:1, one launch (start us, length us, event | category | flops | bytes accessed | tf_op | source)
XLA Modules:
  0.0 61.3 jit_solution(14045483544800398718)
XLA Ops:
  0.6 57.0 %latent_charge.1 = (bf16[8192,256]{1,0:T(8,128)(2,1)}, f32[3,8192]{1,0:T(4,128)}, bf16[2,16,16,256]{3,2,1,0:T(8,128)(2,1)}, f32[8,128]{1,0:T(8,128)}) custom-call(bf16[8192,256]{1,0:T(8,128)(2,1)} %feat.1, f32[3,8192]{1,0:T(4,128)} %refs_0_.1, f32[1,8192]{1,0:T(1,128)} %bitcast.13, s32[1,8192]{1,0:T(1,128)} %bitcast.14, s32[64,128]{1,0:T(8,128)} %bitcast.15, ...), custom_call_target="tpu_custom_call" | custom-call | tf_op jit(solution)/shard_map/latent_charge/pallas_call | solution.py:592
  57.7 3.6 %results.1 = (bf16[8192,256]{1,0:T(8,128)(2,1)}, f32[3,8192]{1,0:T(4,128)}, f32[256,256]{1,0:T(8,128)}, f32[1,256]{1,0:T(1,128)}, f32[256,256]{1,0:T(8,128)}, /*index=5*/f32[1,256]{1,0:T(1,128)}, f32[1,256]{1,0:T(1,128)}) custom-call(bf16[8192,256]{1,0:T(8,128)(2,1)} %get-tuple-element.18.fgrad, f32[3,8192]{1,0:T(4,128)} %get-tuple-element.19.pgrad, ...), custom_call_target="tpu_custom_call" | custom-call | tf_op jit(solution)/shard_map/results/pallas_call | solution.py:604

commit v4 on v3

--- a/solution.py
+++ b/solution.py
@@ -13,7 +13,7 @@
 COUPLING = 0.5
 SLOT_DEV = 128
 HEAD_CHUNK = 1024
-CHUNK = 2048
+CHUNK = 4096
 NT = (((1,), (1,)), ((), ()))
 NN = (((1,), (0,)), ((), ()))
 TN = (((0,), (0,)), ((), ()))
@@ -44,7 +44,11 @@
 
 
 def shift_x(x):
-    first = roll(pltpu.roll(x, 120, 1, stride=1, stride_axis=0), 6)
+    return wrap_x(roll(pltpu.roll(x, 120, 1, stride=1, stride_axis=0), 6))
+
+
+def wrap_x(first):
+    x = first
     col = iota(x.shape, 1) % 8 + 2 - iota(x.shape, 0)
     return jnp.where(col > 7, roll(first, 8), jnp.where(col < 0, roll(first, -8), first))
 
@@ -61,7 +65,7 @@
     if dz % 2 == 0:
         return slabs[dz // 2 + 1]
     low, high = (0, 1) if dz == -1 else (1, 2)
-    lower = iota(slabs[1].shape, 1) < 64
+    lower = iota(slabs[low].shape, 1) < 64
     return jnp.where(lower, roll(slabs[low], 64), roll(slabs[high], 64))
 
 
@@ -76,8 +80,8 @@
     )
     fgrad, pgrad, mats, bias_out = outs
     (
-    X, A1, SL1, A2, SL2, OB, OD, BLK, U, Q, W1H, W1T, W2TH, W2H, B1, B2, WO,
-    CODE, CA, CB, CS, F, G, GN, R, LCODE, MACC, MX, P1, S1, P2, TO, TB,
+    X, A1, SL1, A2, SL2, OB, OD, BLK, U, Q, W1H, W1T, W2TH, W2H, B1, B2, WO, WOH,
+    CODE, CA, CB, CS, F, G, GN, R, LCODE, LN, MACC, MX, P1, TO, TX, TC, TB,
     ACC, OGACC, IBACC, BOTH, RX, SB, RM, GS, GM, AS, AM, AO,
     BV, BX, BC, BL, BS, BG, BF, GR, FIELD, PG,
     xsem, osem, isem, ssem, rsem,
@@ -97,7 +101,6 @@
     n_z = n_graph // 2
     n_heads = atoms // head_chunk
     n_chunks = atoms // chunk
-    half_grp = 2 * (n_grp // 5)
 
     def leaf_peer(o):
         return lax.rem(l + o, n_leaf)
@@ -124,6 +127,14 @@
         @pl.loop(1, n_z)
         def _(o):
             send(k, src, dst, (lax.rem(g + 2 * o, n_graph), l))
+
+    def to_chips(k, src, dst):
+        mine = zpos * n_leaf + l
+
+        @pl.loop(1, n_z * n_leaf)
+        def _(o):
+            chip = lax.rem(mine + o, n_z * n_leaf)
+            send(k, src, dst, (2 * (chip // n_leaf) + core, lax.rem(chip, n_leaf)))
 
     def to_core(k, src, dst):
         send(k, src, dst, (g + 1 - 2 * core, l))
@@ -186,7 +197,9 @@
     B1[...] = column(0.5 * b_in[...])
     B2[...] = column(0.5 * b_mid[...])
     for i in range(hid // 128):
-        WO[128 * i : 128 * i + 128, :] = column(w_out[i : i + 1, :].astype(F32))
+        wo = column(w_out[i : i + 1, :].astype(F32))
+        WO[128 * i : 128 * i + 128, :] = wo
+        WOH[128 * i : 128 * i + 128, :] = 0.5 * wo
     A1[hid:, :] = jnp.ones((A1.shape[0] - hid, atoms), BF16)
     U[...] = jnp.ones_like(U)
     U[1:4, :] = pos[...]
@@ -200,22 +213,6 @@
         for i, coord in enumerate([lambda b: b & 7, lambda b: (b >> 3) & 7, lambda b: b >> 6])
     ]
     LCODE[...] = ((dz + 2) * 5 + dy + 2) * 8 + 2 - dx
-    sub = iota((8, 128), 0)
-
-    def mask_step(k, masks):
-        row = LCODE[pl.ds(k, 1), :] - sub
-        return tuple(m + jnp.where(row == 8 * i, 1.0, 0.0) for i, m in enumerate(masks))
-
-    masks = lax.fori_loop(
-        0, lbox.shape[0], mask_step, tuple(jnp.zeros((8, 128), F32) for _ in range(n_grp)), unroll=4
-    )
-    G[...] = jnp.zeros_like(G)
-    for i in range(n_grp):
-        F[8 * i : 8 * i + 8, :] = masks[i]
-    for i in range(n_grp):
-        for j in range(5):
-            other = 8 * (n_grp - 1 - i) + 4 - j
-            G[8 * i + j : 8 * i + j + 1, :] = F[other : other + 1, :]
 
     def scale_row(cols):
         return (0.5 * COUPLING) * ew[:, cols]
@@ -237,24 +234,21 @@
         wo = tile_lanes(WO[...], head_chunk)
         a = h + h * t
         Q[:, at] = jnp.sum(a * wo, 0, keepdims=True)
-        a = a.astype(BF16)
-        A2[:, at] = a
-        t = t.astype(BF16)
-        SL2[:, at] = ((1 + a) + t * (1 - a)) * (0.5 * wo).astype(BF16)
+        A2[:, at] = a.astype(BF16)
+        half_wo = tile_lanes(WOH[...], head_chunk)
+        SL2[:, at] = (((1.0 + a) + t * (1.0 - a)) * half_wo).astype(BF16)
 
     def before_place(c):
         cols = pl.ds(pl.multiple_of(c * chunk, chunk), chunk)
         s = sslot[:, cols]
         src_leaf = (s >> cap_bits) & (n_leaf - 1)
         row = src_leaf * n_graph + (s >> (cap_bits + leaf_bits))
-        OD[:, cols] = one_hot(row, n_leaf * n_graph)
+        row = row + ((s >> (cap_bits - 1)) & 1) * (n_leaf * n_graph)
+        OD[:, cols] = one_hot(row, 2 * n_leaf * n_graph)
         q = Q[:, cols]
         sub = iota((8, chunk), 0)
         vals = U[:, cols] * jnp.where(sub < 4, q, scale_row(cols) * q)
-        hi = vals.astype(BF16).astype(F32)
-        lo = vals - hi
-        masks = [src_leaf == i for i in range(n_leaf)]
-        blocks = [jnp.where(m, hi, 0.0) for m in masks] + [jnp.where(m, lo, 0.0) for m in masks]
+        blocks = [jnp.where(src_leaf == i, vals, 0.0) for i in range(n_leaf)]
         BLK[:, cols] = jnp.concatenate(blocks, 0).astype(BF16)
 
     def before_grad(c):
@@ -269,9 +263,8 @@
             lambda peer: CODE.at[pl.ds(pl.multiple_of(peer * code_rows, code_rows), code_rows)],
             CA.at[g],
         )
-        rows = 8 * half_grp
-        send(2, G.at[pl.ds(0, rows)], GN.at[0], (g, leaf_peer(1)))
-        send(3, G.at[pl.ds(8 * n_grp - rows, rows)], GN.at[1], (g, leaf_peer(n_leaf - 1)))
+        send(2, LCODE, LN.at[0], (g, leaf_peer(1)))
+        send(3, LCODE, LN.at[1], (g, leaf_peer(n_leaf - 1)))
 
     half = 128 // cap
 
@@ -298,13 +291,13 @@
     mine = codes[:cap]
     for i in range(1, half):
         mine = jnp.where(lax.rem(l, half) == i, codes[i * cap : (i + 1) * cap], mine)
-    mine = mine.astype(BF16)
+    mine = jnp.concatenate([mine[: cap // 2], mine[cap // 2 :]], 1).astype(BF16)
     MACC[...] = jnp.zeros_like(MACC)
 
     def place(c):
         cols = pl.ds(pl.multiple_of(c * chunk, chunk), chunk)
         picked = mm(mine, OD[:, cols])
-        in_row = iota((cap, chunk), 0) == (sslot[:, cols] & (cap - 1))
+        in_row = iota((cap // 2, chunk), 0) == (sslot[:, cols] & (cap // 2 - 1))
         atom_box = jnp.sum(jnp.where(in_row, picked, 0.0), 0, keepdims=True)
         ob = one_hot(atom_box.astype(jnp.int32), box_dev)
         OB[:, cols] = ob
@@ -313,44 +306,63 @@
     pl.loop(0, n_chunks)(place)
 
     rows = n_leaf * 8
-    part = MACC[:rows, :] + MACC[rows:, :]
+    part = MACC[...]
     MX[8 : rows + 8, :] = part
     MX[:8, :] = part[rows - 8 :]
     MX[rows + 8 :, :] = part[:8]
     P1[l] = MX[pl.ds(pl.multiple_of(l * 8, 8), 24), :]
     to_leaf(4, lambda peer: MX.at[pl.ds(pl.multiple_of(peer * 8, 8), 24)], P1.at[l])
 
-    wait_on(rsem.at[2], GN.at[0])
-    wait_on(rsem.at[3], GN.at[1])
+    sub = iota((8, 128), 0)
+
+    def build(dst, code_row, groups):
+        def step(k, masks):
+            row = code_row(k) - sub
+            return tuple(m + jnp.where(row == 8 * i, 1.0, 0.0) for i, m in zip(groups, masks))
+
+        zero = tuple(jnp.zeros((8, 128), F32) for _ in groups)
+        masks = lax.fori_loop(0, lbox.shape[0], step, zero, unroll=4)
+        for i, m in zip(groups, masks):
+            dst[8 * i : 8 * i + 8, :] = m
+
+    last = 8 * (n_grp - 1) + 4
+    outer = (n_grp // 5) * 2
+    inner = range(n_grp // 5, n_grp - n_grp // 5)
+    build(F, lambda k: LCODE[pl.ds(k, 1), :], range(n_grp))
+    build(G, lambda k: last - LCODE[pl.ds(k, 1), :], inner)
+    wait_on(rsem.at[2], LN.at[0])
+    wait_on(rsem.at[3], LN.at[1])
+    build(GN.at[0], lambda k: last - LN[0, pl.ds(k, 1), :], range(outer))
+    build(GN.at[1], lambda k: last - LN[1, pl.ds(k, 1), :], range(n_grp - outer, n_grp))
     for i in range(n_grp):
         at = pl.ds(8 * i, 8)
-        slabs = [None, shift_x(G[at, :]), None]
-        if i < half_grp:
-            slabs[0] = shift_x(GN[0, at, :])
-        if i >= n_grp - half_grp:
-            slabs[2] = shift_x(GN[1, pl.ds(8 * (i - n_grp + half_grp), 8), :])
+        slabs = [
+            shift_x(ref[at, :]) if i in used else None
+            for ref, used in (
+                (GN.at[0], range(outer)), (G, inner), (GN.at[1], range(n_grp - outer, n_grp)),
+            )
+        ]
         R[at, :] = shift_y(shift_z(slabs, i // 5 - 2), i % 5 - 2)
     ACC[...] = jnp.zeros_like(ACC)
     OGACC[...] = jnp.zeros_like(OGACC)
     IBACC[...] = jnp.zeros_like(IBACC)
     cut = [n_chunks * i // 4 for i in range(5)]
-    pl.loop(cut[0], cut[2])(before_grad)
+    pl.loop(cut[0], cut[1])(before_grad)
 
     wait_on(rsem.at[4], P1.at[pl.ds(0, n_leaf - 1)])
     total = jnp.sum(P1[...], 0)
-    S1[...] = total
-    P2[g] = total
-    to_graph(5, lambda peer: S1, P2.at[g])
-    pl.loop(cut[2], cut[3])(before_grad)
-    wait_on(rsem.at[5], P2.at[pl.ds(0, n_graph - 1)])
-    total = jnp.sum(P2[...], 0)
-
+
+    total = roll(total, -2)
+    lower = iota((8, 128), 1) < 64
     shifted = []
     for ch in range(8):
-        slabs = [
-            shift_x(jnp.broadcast_to(total[8 * s + ch : 8 * s + ch + 1], (8, 128))) for s in range(3)
-        ]
-        shifted.append([shift_z(slabs, d) for d in range(-2, 3)])
+        planes = []
+        for s in range(3):
+            row = total[8 * s + ch : 8 * s + ch + 1]
+            slab = wrap_x(pltpu.roll(jnp.broadcast_to(row, (8, 128)), 0, 1, stride=1, stride_axis=0))
+            swapped = roll(slab, 64)
+            planes += [jnp.where(lower, slab, swapped), jnp.where(lower, swapped, slab)]
+        shifted.append([[roll(x, -8 * dy) if dy else x for dy in range(-2, 3)] for x in planes])
     off_x = (2 - iota((8, 128), 0)).astype(F32)
     sums = [jnp.zeros((8, 128), F32) for _ in range(8)]
     for i in range(n_grp):
@@ -362,7 +374,8 @@
         for base, mask in ((0, F), (4, R)):
             m = mask[8 * i : 8 * i + 8, :]
             q0, q1, q2, q3 = [
-                m * shift_y(shifted[base + j][off_z + 2], off_y) for j in range(4)
+                m * jnp.where(lower, *(shifted[base + j][off_z + p][off_y + 2] for p in (2, 3)))
+                for j in range(4)
             ]
             proj = off_x * q1 + float(off_y) * q2 + float(off_z) * q3
             sums[base] += q0 * inv - proj * cube
@@ -372,19 +385,22 @@
             sums[base + 3] += (radial * float(off_z) + q3) * cube
     for j in range(8):
         TO[j : j + 1, :] = jnp.sum(sums[j], 0, keepdims=True)
-    TB[l] = TO[...]
-    to_leaf(6, lambda peer: TO, TB.at[l])
-    pl.loop(cut[3], cut[4])(before_grad)
-    wait_on(rsem.at[6], TB.at[pl.ds(0, n_leaf - 1)])
-    table = TB[...].reshape(rows, 128)
+    to_core(5, TO, TX)
+    wait_on(rsem.at[5], TX)
+    TC[...] = TO[...] + TX[...]
+    TB[zpos * n_leaf + l] = TC[...]
+    to_chips(6, TC, TB.at[zpos * n_leaf + l])
+    pl.loop(cut[1], cut[4])(before_grad)
+    wait_on(rsem.at[6], TB.at[pl.ds(0, n_z * n_leaf - 1)])
+    table = jnp.sum(TB[...].reshape(n_z, rows, 128), 0)
     hi = table.astype(BF16)
-    table = jnp.concatenate([hi, (table - hi.astype(F32)).astype(BF16)], 0)
+    table = jnp.concatenate([hi, (table - hi.astype(F32)).astype(BF16)], 1)
 
     def backward(c):
         cols = pl.ds(pl.multiple_of(c * chunk, chunk), chunk)
         src_leaf = (sslot[:, cols] >> cap_bits) & (n_leaf - 1)
-        got = mm(table, OB[:, cols])
-        got = got[:rows] + got[rows:]
+        ob = OB[:, cols]
+        got = mm(table, jnp.concatenate([ob, ob], 0))
         field = jnp.zeros((8, chunk), F32)
         for i in range(n_leaf):
             field += jnp.where(src_leaf == i, got[8 * i : 8 * i + 8], 0.0)
@@ -474,8 +490,8 @@
     graph_sent = pl.ds(0, n_graph - 1)
     z_sent = pl.ds(0, n_z - 1)
     sent = {
-        0: CA.at[graph_sent], 1: CS.at[leaf_sent], 2: GN.at[0], 3: GN.at[1], 4: P1.at[leaf_sent],
-        5: P2.at[graph_sent], 6: TB.at[leaf_sent], 7: RX, 8: BV, 9: RM.at[leaf_sent],
+        0: CA.at[graph_sent], 1: CS.at[leaf_sent], 2: LN.at[0], 3: LN.at[1], 4: P1.at[leaf_sent],
+        5: TX, 6: TB.at[pl.ds(0, n_z * n_leaf - 1)], 7: RX, 8: BV, 9: RM.at[leaf_sent],
         10: BL.at[leaf_sent], 11: GM.at[z_sent], 12: BG.at[z_sent], 13: AM.at[leaf_sent], 14: AO,
     }
     for k, view in sent.items():
@@ -537,7 +553,7 @@
     atoms, feat = features.shape
     hid = w_in.shape[1]
     head_chunk = min(HEAD_CHUNK, atoms // 4)
-    chunk = min(CHUNK, atoms // 4)
+    chunk = min(CHUNK, atoms // 2)
     n_grp = 25
     n_z = n_graph // 2
     code_rows = n_leaf * (atoms // (n_graph * n_leaf)) // 128
@@ -550,17 +566,17 @@
     scratch = [
         v((atoms, feat), BF16), v((hid + 16, atoms), BF16), v((hid, atoms), BF16),
         v((hid, atoms), BF16), v((hid, atoms), BF16), v((128, atoms), BF16),
-        v((n_leaf * n_graph, atoms), BF16), v((n_leaf * 16, atoms), BF16),
+        v((2 * n_leaf * n_graph, atoms), BF16), v((n_leaf * 8, atoms), BF16),
         v((8, atoms)), v((1, atoms)),
         v((hid, feat), BF16), v((hid, feat), BF16), v((hid, hid), BF16), v((hid, hid), BF16),
-        v((hid, 128)), v((hid, 128)), v((hid, 128)),
+        v((hid, 128)), v((hid, 128)), v((hid, 128)), v((hid, 128)),
         v((atoms // 128, 128)), v((n_graph, code_rows, 128)), v((code_rows, n_graph, 128)),
         v((n_leaf, n_graph, 128)),
-        v((8 * n_grp, 128)), v((8 * n_grp, 128)), v((2, 80, 128)), v((8 * n_grp, 128)),
-        v((list_box.shape[1], 128), jnp.int32),
-        v((n_leaf * 16, 128)),
-        v((n_leaf * 8 + 16, 128)), v((n_leaf, 24, 128)), v((24, 128)), v((n_graph, 24, 128)),
-        v((8, 128)), v((n_leaf, 8, 128)),
+        v((8 * n_grp, 128)), v((8 * n_grp, 128)), v((2, 8 * n_grp, 128)), v((8 * n_grp, 128)),
+        v((list_box.shape[1], 128), jnp.int32), v((2, list_box.shape[1], 128), jnp.int32),
+        v((n_leaf * 8, 128)),
+        v((n_leaf * 8 + 16, 128)), v((n_leaf, 24, 128)),
+        v((8, 128)), v((8, 128)), v((8, 128)), v((n_z * n_leaf, 8, 128)),
         v((2, hid + 16, hid)), v((hid, 128)), v((hid, 128)),
         v((2, hid, hid), BF16), v((hid, hid), BF16), v((hid, hid), BF16),
         v((n_leaf, wrow, hid), BF16), v((wrow, hid), BF16), v((n_z, wrow, hid), BF16),

time: 61.4 us -> 58.5 us (0.953)
  Pallas kernels: 60.7 us -> 57.7 us
    pallas_call x1, Pallas kernels: 57 us -> 54.1 us  [body(): pl.pallas_call(functools.partial(kernel, n_graph, n_leaf, head_chunk, chu...]
where the time goes in v4:
time: 58.5 us; the launch traced here: 58.4 us
  Pallas kernels  57.7 us (99%)
  between operations  0.65 us (1%)
    pallas_call x1, Pallas kernels, body(): pl.pallas_call(functools.partial(kernel, n_graph, n_leaf, head_chunk, chu...  54.1 us
    pallas_call x1, Pallas kernels, body(): pl.pallas_call(functools.partial(finish, pieces), out_shape=shapes, in_sp...  3.65 us

profile of v4, /device:TPU:1, one launch (start us, length us, event | category | flops | bytes accessed | tf_op | source)
XLA Modules:
  0.0 58.4 jit_solution(5916482410899009850)
XLA Ops:
  0.6 54.1 %latent_charge.1 = (bf16[8192,256]{1,0:T(8,128)(2,1)}, f32[3,8192]{1,0:T(4,128)}, bf16[2,16,16,256]{3,2,1,0:T(8,128)(2,1)}, f32[8,128]{1,0:T(8,128)}) custom-call(bf16[8192,256]{1,0:T(8,128)(2,1)} %feat.1, f32[3,8192]{1,0:T(4,128)} %refs_0_.1, f32[1,8192]{1,0:T(1,128)} %bitcast.13, s32[1,8192]{1,0:T(1,128)} %bitcast.14, s32[64,128]{1,0:T(8,128)} %bitcast.15, ...), custom_call_target="tpu_custom_call" | custom-call | tf_op jit(solution)/shard_map/latent_charge/pallas_call | solution.py:608
  54.7 3.6 %results.1 = (bf16[8192,256]{1,0:T(8,128)(2,1)}, f32[3,8192]{1,0:T(4,128)}, f32[256,256]{1,0:T(8,128)}, f32[1,256]{1,0:T(1,128)}, f32[256,256]{1,0:T(8,128)}, /*index=5*/f32[1,256]{1,0:T(1,128)}, f32[1,256]{1,0:T(1,128)}) custom-call(bf16[8192,256]{1,0:T(8,128)(2,1)} %get-tuple-element.18.fgrad, f32[3,8192]{1,0:T(4,128)} %get-tuple-element.19.pgrad, ...), custom_call_target="tpu_custom_call" | custom-call | tf_op jit(solution)/shard_map/results/pallas_call | solution.py:620

commit v5 on v4

--- a/solution.py
+++ b/solution.py
@@ -82,7 +82,7 @@
     (
     X, A1, SL1, A2, SL2, OB, OD, BLK, U, Q, W1H, W1T, W2TH, W2H, B1, B2, WO, WOH,
     CODE, CA, CB, CS, F, G, GN, R, LCODE, LN, MACC, MX, P1, TO, TX, TC, TB,
-    ACC, OGACC, IBACC, BOTH, RX, SB, RM, GS, GM, AS, AM, AO,
+    ACC, OGACC, IBACC, BOTH, RX, SB, RM, GS, GM, AS, AM,
     BV, BX, BC, BL, BS, BG, BF, GR, FIELD, PG,
     xsem, osem, isem, ssem, rsem,
     ) = refs
@@ -112,7 +112,7 @@
         ).start()
 
     def to_leaf(k, src_of, dst):
-        @pl.loop(1, n_leaf)
+        @pl.loop(1, n_leaf, unroll=3)
         def _(o):
             peer = leaf_peer(o)
             send(k, src_of(peer), dst, (g, peer))
@@ -131,7 +131,7 @@
     def to_chips(k, src, dst):
         mine = zpos * n_leaf + l
 
-        @pl.loop(1, n_z * n_leaf)
+        @pl.loop(1, n_z * n_leaf, unroll=7 if n_z * n_leaf == 64 else 1)
         def _(o):
             chip = lax.rem(mine + o, n_z * n_leaf)
             send(k, src, dst, (2 * (chip // n_leaf) + core, lax.rem(chip, n_leaf)))
@@ -218,7 +218,8 @@
         return (0.5 * COUPLING) * ew[:, cols]
 
     def one_hot(index, n):
-        return jnp.where(iota((n, chunk), 0) == index, 1.0, 0.0).astype(BF16)
+        hit = iota((n, chunk), 0).astype(BF16) == index.astype(BF16)
+        return jnp.where(hit, BF16(1), BF16(0))
 
     def head(c):
         feat_copy(c).wait()
@@ -482,7 +483,7 @@
     bias_copy = pltpu.make_async_copy(BF, bias_out, isem.at[1])
     bias_copy.start()
     wait_on(rsem.at[13], AM.at[pl.ds(0, n_leaf - 1)])
-    to_core(14, AM, AO)
+    to_core(14, AM, mats.at[core])
     mine_copy = pltpu.make_async_copy(AM, mats.at[core], isem.at[2])
     mine_copy.start()
 
@@ -492,7 +493,7 @@
     sent = {
         0: CA.at[graph_sent], 1: CS.at[leaf_sent], 2: LN.at[0], 3: LN.at[1], 4: P1.at[leaf_sent],
         5: TX, 6: TB.at[pl.ds(0, n_z * n_leaf - 1)], 7: RX, 8: BV, 9: RM.at[leaf_sent],
-        10: BL.at[leaf_sent], 11: GM.at[z_sent], 12: BG.at[z_sent], 13: AM.at[leaf_sent], 14: AO,
+        10: BL.at[leaf_sent], 11: GM.at[z_sent], 12: BG.at[z_sent], 13: AM.at[leaf_sent], 14: AM,
     }
     for k, view in sent.items():
         wait_on(ssem.at[k], view)
@@ -503,11 +504,8 @@
 
     force_copy.wait()
     bias_copy.wait()
-    wait_on(rsem.at[14], AO)
-    other_copy = pltpu.make_async_copy(AO, mats.at[1 - core], isem.at[3])
-    other_copy.start()
     mine_copy.wait()
-    other_copy.wait()
+    wait_on(rsem.at[14], mats.at[1 - core])
 
 
 def finish(
@@ -580,7 +578,7 @@
         v((2, hid + 16, hid)), v((hid, 128)), v((hid, 128)),
         v((2, hid, hid), BF16), v((hid, hid), BF16), v((hid, hid), BF16),
         v((n_leaf, wrow, hid), BF16), v((wrow, hid), BF16), v((n_z, wrow, hid), BF16),
-        v((wrow, hid), BF16), v((n_leaf, wrow, hid), BF16), v((n_leaf, wrow, hid), BF16),
+        v((wrow, hid), BF16), v((n_leaf, wrow, hid), BF16),
         v((8, 128)), v((2, 8, 128)), v((8, 128)), v((n_leaf, 8, 128)), v((8, 128)),
         v((n_z, 8, 128)), v((8, 128)), v((16, atoms), BF16), v((8, atoms)), v((3, atoms)),
         pltpu.SemaphoreType.DMA((atoms // head_chunk,)), pltpu.SemaphoreType.DMA((atoms // chunk,)),

time: 58.5 us -> 57.4 us (0.981)
  Pallas kernels: 57.7 us -> 56.7 us
    pallas_call x1, Pallas kernels: 54.1 us -> 53 us  [body(): pl.pallas_call(functools.partial(kernel, n_graph, n_leaf, head_chunk, chu...]
where the time goes in v5:
time: 57.4 us; the launch traced here: 57.3 us
  Pallas kernels  56.7 us (99%)
  between operations  0.65 us (1%)
    pallas_call x1, Pallas kernels, body(): pl.pallas_call(functools.partial(kernel, n_graph, n_leaf, head_chunk, chu...  53 us
    pallas_call x1, Pallas kernels, body(): pl.pallas_call(functools.partial(finish, pieces), out_shape=shapes, in_sp...  3.65 us

profile of v5, /device:TPU:1, one launch (start us, length us, event | category | flops | bytes accessed | tf_op | source)
XLA Modules:
  0.0 57.3 jit_solution(17070920331182730787)
XLA Ops:
  0.6 53.0 %latent_charge.1 = (bf16[8192,256]{1,0:T(8,128)(2,1)}, f32[3,8192]{1,0:T(4,128)}, bf16[2,16,16,256]{3,2,1,0:T(8,128)(2,1)}, f32[8,128]{1,0:T(8,128)}) custom-call(bf16[8192,256]{1,0:T(8,128)(2,1)} %feat.1, f32[3,8192]{1,0:T(4,128)} %refs_0_.1, f32[1,8192]{1,0:T(1,128)} %bitcast.13, s32[1,8192]{1,0:T(1,128)} %bitcast.14, s32[64,128]{1,0:T(8,128)} %bitcast.15, ...), custom_call_target="tpu_custom_call" | custom-call | tf_op jit(solution)/shard_map/latent_charge/pallas_call | solution.py:606
  53.7 3.6 %results.1 = (bf16[8192,256]{1,0:T(8,128)(2,1)}, f32[3,8192]{1,0:T(4,128)}, f32[256,256]{1,0:T(8,128)}, f32[1,256]{1,0:T(1,128)}, f32[256,256]{1,0:T(8,128)}, /*index=5*/f32[1,256]{1,0:T(1,128)}, f32[1,256]{1,0:T(1,128)}) custom-call(bf16[8192,256]{1,0:T(8,128)(2,1)} %get-tuple-element.18.fgrad, f32[3,8192]{1,0:T(4,128)} %get-tuple-element.19.pgrad, ...), custom_call_target="tpu_custom_call" | custom-call | tf_op jit(solution)/shard_map/results/pallas_call | solution.py:618
